TPU v7x, 256 devices: a whole 4x4x8 slice. The times are simulated.
256 devices in a mesh: dom: 16 (over x, y), orb: 16 (over z, core).
Axes of the slice: x: 4, y: 4, z: 8, core: 2. Of those that a mesh axis runs over, the one named last changes fastest.
Arguments:
- orbitals: float32 [256, 128, 16, 128], P('orb', 'dom'), may hold values from -6 to 6
- potential: float32 [128, 16, 128], P('dom'), may hold values from 0.2 to 17, as said below
- rotation: float32 [256, 256], P('orb'), may hold values from -0.6 to 0.6
- block: int32 [1], replicated, may hold values from 0 to 15
- owner: int32 [1], replicated, may hold values from 0 to 15
Outputs:
- gradient: float32 [16, 128, 16, 128], P(None, 'dom')
- updated: float32 [256, 128, 16, 128], P('orb', 'dom')
Inputs may be any that keep to these rules, and one draw needn't show every extreme that they name: A positive local potential.
All inputs are finite; a program needn't handle non-finite values.
Results may differ from a plain program's by a relative error of at most 0.00017.
Values sent between devices are 32-bit elements; how exact they have to be, the bound alone decides.
A program may use at most 128 MiB of HBM per device.

v0:
```python
import jax
import jax.numpy as jnp
from jax import lax
from jax.sharding import PartitionSpec as P

CENTER = -5369.0 / 1800.0
SIDES = (12.0 / 7.0, -15.0 / 56.0, 10.0 / 189.0, -1.0 / 112.0, 2.0 / 1925.0, -1.0 / 16632.0)


def padded_2(value, sides, width):
    for axis, dim in sides:
        count, length = (lax.axis_size(axis), value.shape[dim])
        up = [(i, (i + 1) % count) for i in range(count)]
        down = [(j, i) for i, j in up]
        last = lax.slice_in_dim(value, length - width, length, axis=dim)
        leading = lax.slice_in_dim(value, 0, width, axis=dim)
        before = lax.ppermute(last, axis, up)
        after = lax.ppermute(leading, axis, down)
        value = jnp.concatenate([before, value, after], axis=dim)
    return value


def from_root(value, axis, root):
    mine = lax.axis_index(axis) == root
    return lax.psum(jnp.where(mine, value, jnp.zeros_like(value)), axis)


def hamiltonian(field, potential):
    planes = field.shape[1]
    padded = padded_2(field, (("dom", 1),), 6)
    summed = 3.0 * CENTER * field
    for offset in range(1, 7):
        weight = SIDES[offset - 1]
        upper = padded[:, 6 + offset : 6 + offset + planes]
        lower = padded[:, 6 - offset : 6 - offset + planes]
        summed = summed + weight * (upper + lower)
        for axis_pos in (2, 3):
            summed = summed + weight * (
                jnp.roll(field, offset, axis_pos) + jnp.roll(field, -offset, axis_pos)
            )
    return -0.5 * summed + potential[None] * field


def per_device(orbitals, potential, rotation, block, owner):
    blk_size = orbitals.shape[0]
    planes = orbitals.shape[1]
    rows_y = orbitals.shape[2]
    rows_z = orbitals.shape[3]
    volume = 1.0 / (planes * lax.axis_size("dom") * rows_y * rows_z)
    block_root = block[0]
    device_rank = lax.axis_index("orb")
    active = from_root(orbitals, "orb", block_root)
    applied = hamiltonian(active, potential)
    partial_value = (
        jnp.einsum("axyz,cxyz->ac", orbitals, applied, precision=lax.Precision.HIGHEST) * volume
    )
    proj = lax.psum(partial_value, "dom")
    local_term = jnp.einsum("axyz,ac->cxyz", orbitals, proj, precision=lax.Precision.HIGHEST)
    removed = lax.psum(local_term, "orb")
    gradient = applied - removed
    full_panel = from_root(rotation, "orb", owner[0])
    panel_piece = lax.dynamic_slice_in_dim(full_panel, device_rank * blk_size, blk_size, 1)
    added = jnp.einsum("cxyz,ca->axyz", gradient, panel_piece, precision=lax.Precision.HIGHEST)
    updated = orbitals + added
    return (gradient, updated)


def solution(mesh):
    in_specs = (P("orb", "dom", None, None), P("dom", None, None), P("orb", None), P(), P())
    out_specs = (P(None, "dom", None, None), P("orb", "dom", None, None))
    return jax.shard_map(
        per_device, mesh=mesh, in_specs=in_specs, out_specs=out_specs, check_vma=False
    )
```

profile of v0, /device:TPU:1, one launch (start us, length us, event | category | flops | bytes accessed | tf_op | source)
XLA Modules:
  0.0 348.1 jit_solution(13830886444404603520)
XLA Ops:
  7.2 0.0 all-reduce.3.cloned.1.call-start
  7.9 2.9 copy_select_fusion
  10.7 0.0 all-reduce.3.cloned.1.call-update
  10.8 0.0 all-reduce.5.cloned.1.call-start
  10.8 115.3 %all-reduce.3.cloned.1.call-done = f32[16,8,16,128]{3,0,2,1:T(8,128)} async-done(((f32[16,8,16,128]{3,0,2,1:T(8,128)}), f32[16,8,16,128]{3,0,2,1:T(8,128)}) %all-reduce.3.cloned.1.call-update) | async-done | bytes 1048592 | tf_op jit(solution)/shard_map/psum | solution.py:25
  126.1 0.0 copy-start
  126.1 1.6 fusion.71
  127.7 1.3 collective-permute-start.1
  129.0 3.7 %collective-permute-start = (f32[16,6,16,128]{3,0,2,1:T(8,128)S(1)}, f32[16,6,16,128]{3,0,2,1:T(8,128)S(1)}, u32[]{:S(2)}, u32[]{:S(2)}) collective-permute-start(f32[16,6,16,128]{3,0,2,1:T(8,128)S(1)} %get-tuple-element.54), channel_id=1, source_target_pairs={{16,0},{32,16},{48,32},{64,48},{80,64},{96,80},{112,96},{128,112},... | collective-permute-start | bytes 2359304 | tf_op jit(solution)/shard_map/ppermute | solution.py:18
  132.7 0.0 copy-done
  132.7 1.7 fusion.51
  134.3 1.7 fusion.52
  136.0 1.6 fusion.55
  137.7 1.6 fusion.56
  139.3 1.7 fusion.59
  141.0 1.8 fusion.60
  142.8 1.7 fusion.63
  144.4 1.7 fusion.64
  146.2 1.7 fusion.67
  147.8 1.7 fusion.68
  149.5 1.7 fusion.47
  151.2 1.4 fusion.69
  152.6 1.5 fusion.65
  154.1 1.3 fusion.61
  155.4 1.3 fusion.57
  156.7 1.2 fusion.53
  157.9 1.0 fusion.49
  159.0 0.9 fusion.54
  159.8 0.9 fusion.58
  160.7 0.8 fusion.62
  161.5 0.7 fusion.66
  162.2 1.0 fusion.50
  163.2 0.6 fusion.70
  163.8 1.7 fusion.48
  165.6 0.0 collective-permute-done.1
  165.6 0.1 constant_dynamic-update-slice_fusion.3
  165.7 0.2 constant_dynamic-update-slice_fusion.1
  165.9 0.0 copy-start.1
  165.9 0.0 collective-permute-done
  165.9 0.1 constant_dynamic-update-slice_fusion
  166.0 1.2 copy-done.1
  167.1 17.6 %fusion.7 = f32[16,8,16,128]{3,0,2,1:T(8,128)} fusion(f32[16,14,16,128]{3,0,2,1:T(8,128)} %copy-done.1, f32[16,14,16,128]{3,0,2,1:T(8,128)S(1)} %constant_dynamic-update-slice_fusion, f32[16,8,15,128]{3,0,2,1:T(8,128)} %get-tuple-element.51, f32[16,8,1,128]{3,0,2,1:T(8,128)} %get-tuple-element.53, f32[16,8,1,128]{3,0,2,1:T(8,128)} %get-tuple-element.52, ...), kind=kLoop, calls=%fused_computation.10 | loop fusion | flops 21495808 | bytes 39911424 | tf_op jit(solution)/shard_map/add | solution.py:41
  184.7 0.0 copy-start.2
  184.7 3.4 fusion.1
  188.1 0.0 copy-start.4
  188.2 0.0 copy-start.3
  188.2 30.3 %psum.29 = f32[16,16]{0,1:T(8,128)S(1)} all-reduce(f32[16,16]{0,1:T(8,128)S(1)} %fusion.1), channel_id=1, replica_groups=mesh['dom'=16,'orb'=16] {'dom'}, use_global_device_ids=true, to_apply=%region_1.2 | all-reduce | flops 256 | bytes 2048 | tf_op jit(solution)/shard_map/psum | solution.py:57
  218.5 0.0 copy-done.2
  218.5 2.5 fusion.41
  221.0 0.0 all-reduce.5.cloned.1.call-update
  221.6 0.0 copy-done.4
  221.7 51.0 %psum.31 = f32[16,256]{1,0:T(8,128)S(1)} all-reduce(f32[16,256]{1,0:T(8,128)S(1)} %broadcast_select_fusion), channel_id=1, replica_groups=mesh['dom'=16,'orb'=16] {'orb'}, use_global_device_ids=true, to_apply=%region_3.4 | all-reduce | flops 4096 | bytes 32768 | tf_op jit(solution)/shard_map/psum | solution.py:25
  272.7 63.0 %all-reduce.5.cloned.1.call-done = f32[16,8,16,128]{3,0,2,1:T(8,128)} async-done(((f32[16,8,16,128]{3,0,2,1:T(8,128)}), f32[16,8,16,128]{3,0,2,1:T(8,128)}) %all-reduce.5.cloned.1.call-update) | async-done | bytes 1048592 | tf_op jit(solution)/shard_map/psum | solution.py:59
  335.7 0.0 copy-done.3
  335.7 1.4 sub.3
  337.1 1.3 copy.19
  338.3 1.6 convolution_add_fusion
  340.0 1.3 copy.20
  (1 shorter events, 0.0 us)
Async XLA Ops:
  7.2 119.0 %all-reduce.3.cloned.1.call-start = ((), (), s32[]{:S(2)}) async-start(), calls=%async_computation | async-start | bytes 2097152 | tf_op jit(solution)/shard_map/psum | solution.py:25
  10.8 324.9 %all-reduce.5.cloned.1.call-start = ((), (), s32[]{:S(2)}) async-start(), calls=%async_computation.1 | async-start | bytes 2097152 | tf_op jit(solution)/shard_map/psum | solution.py:59
  126.1 6.5 %copy-start = (f32[16,8,16,128]{3,0,2,1:T(8,128)S(1)}, f32[16,8,16,128]{3,0,2,1:T(8,128)}, u32[]{:S(2)}) copy-start(f32[16,8,16,128]{3,0,2,1:T(8,128)} %all-reduce.3.cloned.1.call-done) | copy-start | bytes 3145732
  127.7 37.9 %collective-permute-start.1 = (f32[16,6,16,128]{3,0,2,1:T(8,128)S(1)}, f32[16,6,16,128]{3,0,2,1:T(8,128)S(1)}, u32[]{:S(2)}, u32[]{:S(2)}) collective-permute-start(f32[16,6,16,128]{3,0,2,1:T(8,128)S(1)} %get-tuple-element.55), channel_id=1, source_target_pairs={{0,16},{16,32},{32,48},{48,64},{64,80},{80,96},{96,112},{112,128},... | collective-permute-start | bytes 2359304 | tf_op jit(solution)/shard_map/ppermute | solution.py:17
  129.0 36.9 %collective-permute-start = (f32[16,6,16,128]{3,0,2,1:T(8,128)S(1)}, f32[16,6,16,128]{3,0,2,1:T(8,128)S(1)}, u32[]{:S(2)}, u32[]{:S(2)}) collective-permute-start(f32[16,6,16,128]{3,0,2,1:T(8,128)S(1)} %get-tuple-element.54), channel_id=1, source_target_pairs={{16,0},{32,16},{48,32},{64,48},{80,64},{96,80},{112,96},{128,112},... | collective-permute-start | bytes 2359304 | tf_op jit(solution)/shard_map/ppermute | solution.py:18
  165.9 1.3 copy-start.1
  184.7 33.8 %copy-start.2 = (f32[16,8,16,128]{3,2,1,0:T(8,128)S(1)}, f32[16,8,16,128]{3,2,1,0:T(8,128)}, u32[]{:S(2)}) copy-start(f32[16,8,16,128]{3,2,1,0:T(8,128)} %param.5) | copy-start | bytes 3145732
  188.1 33.5 %copy-start.4 = (f32[16,256]{1,0:T(8,128)S(1)}, f32[16,256]{1,0:T(8,128)}, u32[]{:S(2)}) copy-start(f32[16,256]{1,0:T(8,128)} %param.7) | copy-start | bytes 49156
  188.2 147.5 %copy-start.3 = (f32[16,8,16,128]{3,0,2,1:T(8,128)S(1)}, f32[16,8,16,128]{3,0,2,1:T(8,128)}, u32[]{:S(2)}) copy-start(f32[16,8,16,128]{3,0,2,1:T(8,128)} %fusion.7) | copy-start | bytes 3145732
Sparse Core Ops, SparseCore 0:
  10.9 115.1 all-reduce.2
  221.1 114.5 all-reduce.4
where the time goes:
time: 348 us
  waiting for transfers between devices  178 us (51%)
  blocking collectives  81.3 us (23%)
  local copies, waits for them, and re-layouts  38.6 us (11%)
  other arithmetic  21.8 us (6%)
  between operations  15.5 us (4%)
  matrix products  7.46 us (2%)
  starting transfers between devices  5.02 us (1%)
    psum x1, waiting for transfers between devices, from_root(): return lax.psum(jnp.where(mine, value, jnp.zeros_like(value)), axis)  115 us
    psum x1, waiting for transfers between devices, per_device(): removed = lax.psum(local_term, 'orb')  63 us
    psum x1, blocking collectives, from_root(): return lax.psum(jnp.where(mine, value, jnp.zeros_like(value)), axis)  51 us
    slice x24, local copies, waits for them, and re-layouts, hamiltonian(): jnp.roll(field, -offset, axis_pos)  32.9 us
    psum x1, blocking collectives, per_device(): proj = lax.psum(partial_value, 'dom')  30.3 us
    add x1, other arithmetic, hamiltonian(): return -0.5 * summed + potential[None] * field  17.6 us
  transfers between devices with their start and end apart: 4, of which 2 were waited for; matrix products, arithmetic and copies ran while one was open for 10% of the time, Pallas kernels for 0%

commit v1 on v0

v1 whole, which is shorter than its diff:
```python
import functools

import jax
import jax.numpy as jnp
from jax import lax
from jax.experimental import pallas as pl
from jax.experimental.pallas import tpu as pltpu
from jax.sharding import PartitionSpec as P

CENTER = -5369.0 / 1800.0
SIDES = (12.0 / 7.0, -15.0 / 56.0, 10.0 / 189.0, -1.0 / 112.0, 2.0 / 1925.0, -1.0 / 16632.0)

MESH = pl.DeviceIdType.MESH
NB = 16
NX, NY, NZ = 8, 16, 128
NDOM, NORB, NCHIP = 16, 16, 8
HALO = 6
LO, HI, ALL = (0, 4), (4, 4), (0, 8)
BF = jnp.bfloat16
F32 = jnp.float32


def split(value):
    high = value.astype(BF)
    return high, (value - high.astype(F32)).astype(BF)


def dot_nt(a, b):
    return lax.dot_general(a, b, (((1,), (1,)), ((), ())), preferred_element_type=F32)


def dot_nn(a, b):
    return lax.dot_general(a, b, (((1,), (0,)), ((), ())), preferred_element_type=F32)


def exact_dot(a, b):
    return lax.dot_general(
        a, b, (((1,), (0,)), ((), ())), preferred_element_type=F32, precision=lax.Precision.HIGHEST
    )


def indicator(shape, row_of, col_of):
    rows = lax.broadcasted_iota(jnp.int32, shape, 0)
    cols = lax.broadcasted_iota(jnp.int32, shape, 1)
    return row_of(rows) == col_of(cols)


def kernel(
    block_ref, owner_ref, x_hbm, pot_hbm, rot_hbm, grad_hbm, upd_hbm,
    x2, xh, xl, pot, rot, mask, remo, act, ham, amat, grad, upd, pbuf, panels,
    a1, a2, d1, b2, sb, send, recv, loc,
):
    dom = lax.axis_index("dom")
    orb = lax.axis_index("orb")
    z = lax.div(orb, 2)
    q = lax.rem(orb, 2)

    def chip(k):
        return lax.rem(z + (k + NCHIP), NCHIP)

    def peer(k):
        return (dom, 2 * chip(k) + q)

    def side(k):
        return (lax.rem(dom + (k + NDOM), NDOM), orb)

    sibling = (dom, orb + 1 - 2 * q)
    sems = iter(range(send.shape[0]))
    started = []

    def remote(src, dst, device):
        i = next(sems)
        copy = pltpu.make_async_remote_copy(
            src_ref=src, dst_ref=dst, send_sem=send.at[i], recv_sem=recv.at[i],
            device_id=device, device_id_type=MESH,
        )
        copy.start()
        started.append(copy)
        return copy

    load_x = pltpu.make_async_copy(x_hbm, x2.at[q], loc.at[0])
    load_pot = pltpu.make_async_copy(pot_hbm, pot, loc.at[1])
    load_rot = pltpu.make_async_copy(rot_hbm, rot, loc.at[2])
    for copy in (load_x, load_pot, load_rot):
        copy.start()
    barrier = pltpu.get_barrier_semaphore()
    for k in range(1, NDOM):
        pl.semaphore_signal(barrier, inc=1, device_id=side(k), device_id_type=MESH)
    for k in range(1, NORB):
        pl.semaphore_signal(
            barrier, inc=1, device_id=(dom, lax.rem(orb + k, NORB)), device_id_type=MESH
        )
    for copy in (load_x, load_pot, load_rot):
        copy.wait()
    pl.semaphore_wait(barrier, NDOM + NORB - 2)

    twin = []
    for parity in (1 - q, q):
        twin.append([
            remote(x2.at[q, 2 * s + parity], x2.at[q, 2 * s + parity], sibling)
            for s in range(NCHIP)
        ])

    def reduce_scatter(part, slot):
        def cut(ref, *lead, half=ALL):
            return ref.at[(*lead, pl.ds(*half))]

        def first(sign, half):
            src = cut(part, chip(3 * sign), half=half)
            return remote(src, cut(a1, slot, (1 - sign) // 2, half=half), peer(sign))

        def far(sign, half):
            return remote(cut(part, chip(4), half=half), a2.at[slot, (1 - sign) // 2], peer(2 * sign))

        def near(sign):
            return remote(part.at[chip(sign)], d1.at[slot, (1 - sign) // 2], peer(sign))

        def second(sign, half, arrivals, with_far):
            i = (1 - sign) // 2
            for copy in arrivals:
                copy.wait_recv()
            rows = slice(half[0], half[0] + half[1])
            total = part[chip(2 * sign), rows] + a1[slot, i, rows]
            if with_far:
                total = total + a2[slot, i]
            sb[slot, i, rows] = total
            return remote(
                cut(sb, slot, i, half=half), cut(b2, slot, i, half=half), peer(2 * sign)
            )

        p_hi, m_lo = first(1, HI), first(-1, LO)
        p_far, m_far = far(1, LO), far(-1, HI)
        p_lo, m_hi = first(1, LO), first(-1, HI)
        nears = [near(1), near(-1)]
        last = [
            second(1, HI, [p_hi], False),
            second(-1, LO, [m_lo], False),
            second(1, LO, [p_far, p_lo], True),
            second(-1, HI, [m_far, m_hi], True),
        ]
        for copy in nears + last:
            copy.wait_recv()
        return part[z] + (d1[slot, 0] + d1[slot, 1]) + (b2[slot, 0] + b2[slot, 1])

    def all_gather(buf, index, arrived=lambda k: None):
        def forward(k, half, to):
            ref = buf.at[index(k), pl.ds(*half)]
            return remote(ref, ref, peer(to))

        p_lo, m_hi = forward(0, LO, 2), forward(0, HI, -2)
        p_hi, m_lo = forward(0, HI, 2), forward(0, LO, -2)
        p_near, m_near = forward(0, ALL, 1), forward(0, ALL, -1)
        arrived(0)
        p_lo.wait_recv()
        p_far, p_3lo = forward(-2, LO, 2), forward(-2, LO, 1)
        m_hi.wait_recv()
        m_far, m_3hi = forward(2, HI, -2), forward(2, HI, -1)
        p_hi.wait_recv()
        p_3hi = forward(-2, HI, 1)
        arrived(-2)
        m_lo.wait_recv()
        m_3lo = forward(2, LO, -1)
        arrived(2)
        for k, copies in (
            (-1, (p_near,)), (1, (m_near,)), (-3, (p_3lo, p_3hi)), (3, (m_3hi, m_3lo)), (4, (p_far, m_far)),
        ):
            for copy in copies:
                copy.wait_recv()
            arrived(k)

    block = block_ref[0]
    root_chip = lax.div(block, 2)
    root_core = lax.rem(block, 2)
    is_root = root_chip == z
    for copy in twin[0]:
        copy.wait_recv()
    for s in range(NCHIP):
        mine = jnp.where(root_core == 0, x2[0, 2 * s + q], x2[1, 2 * s + q])
        mask[s] = jnp.where(is_root, mine, 0.0)
    act[pl.ds(HALO, NX)] = reduce_scatter(mask, 0)

    up = remote(act.at[pl.ds(NX, HALO)], act.at[pl.ds(0, HALO)], side(1))
    down = remote(act.at[pl.ds(HALO, HALO)], act.at[pl.ds(HALO + NX, HALO)], side(-1))

    half = pl.ds(pl.multiple_of(lax.div(orb, 8) * 128, 128), 128)
    panel_copies = []
    for k in range(1, NORB):
        to = lax.rem(orb + k, NORB)
        cols = pl.ds(pl.multiple_of(lax.div(to, 8) * 128, 128), 128)
        panel_copies.append(remote(rot.at[:, cols], panels.at[orb], (dom, to)))
    panels[orb] = rot[:, half]

    field = act[pl.ds(HALO, NX)]
    inner = (pot[...] - 1.5 * CENTER) * field
    for k in range(1, 7):
        near = (
            pltpu.roll(field, k, 1) + pltpu.roll(field, NY - k, 1)
            + pltpu.roll(field, k, 2) + pltpu.roll(field, NZ - k, 2)
        )
        inner = inner - (0.5 * SIDES[k - 1]) * near
    up.wait_recv()
    down.wait_recv()
    for k in range(1, 7):
        inner = inner - (0.5 * SIDES[k - 1]) * (act[pl.ds(HALO + k, NX)] + act[pl.ds(HALO - k, NX)])
    ham[...] = inner
    amat[z] = inner

    for copy in twin[1]:
        copy.wait_recv()
    for j in range(2):
        def cast(a, carry, j=j):
            high, low = split(x2[j, a])
            xh[j, a] = high
            xl[j, a] = low
            return carry
        lax.fori_loop(0, NB, cast, 0)
    all_gather(amat, chip)

    rows, cols = NCHIP * NY, 2 * NB * NY
    same_y = indicator((rows, cols), lambda r: r & (NY - 1), lambda c: c & (NY - 1))
    gram = jnp.zeros((rows, cols), F32)
    for x in range(0, NX, 2):
        a_pair = jnp.concatenate([amat[:, x].reshape(rows, NZ), amat[:, x + 1].reshape(rows, NZ)], 1)
        h_pair, l_pair = (
            jnp.concatenate([r[:, :, x].reshape(cols, NZ), r[:, :, x + 1].reshape(cols, NZ)], 1)
            for r in (xh, xl)
        )
        a_high, a_low = split(a_pair)
        both = dot_nt(jnp.concatenate([a_high, a_low], 0), h_pair)
        gram = gram + (both[:rows] + both[rows:] + dot_nt(a_high, l_pair))
    summed = jnp.where(same_y, gram, 0.0).reshape(NCHIP, NY, cols).sum(1)
    of_orbital = jnp.where(indicator((cols, 128), lambda r: r // NY, lambda c: c), 1.0, 0.0)
    pbuf[dom] = exact_dot(summed, of_orbital)
    exchange = [remote(pbuf.at[dom], pbuf.at[dom], side(k)) for k in range(1, NDOM)]
    for copy in exchange:
        copy.wait_recv()
    proj = pbuf[...].sum(0) * (1.0 / (NX * NDOM * NY * NZ))

    to_rows = jnp.where(indicator((128, cols), lambda r: r, lambda c: c // NY), 1.0, 0.0)
    spread = exact_dot(proj, to_rows)
    spread = jnp.broadcast_to(spread[:, None, :], (NCHIP, NY, cols)).reshape(rows, cols)
    k_high, k_low = split(jnp.where(same_y, spread, 0.0))
    k_both = jnp.concatenate([k_high, k_low], 0)
    for x in range(0, NX, 2):
        h_pair, l_pair = (
            jnp.concatenate([r[:, :, x].reshape(cols, NZ), r[:, :, x + 1].reshape(cols, NZ)], 1)
            for r in (xh, xl)
        )
        both = dot_nn(k_both, h_pair)
        part = both[:rows] + both[rows:] + dot_nn(k_high, l_pair)
        remo[:, x] = part[:, :NZ].reshape(NCHIP, NY, NZ)
        remo[:, x + 1] = part[:, NZ:].reshape(NCHIP, NY, NZ)
    grad[orb] = ham[...] - reduce_scatter(remo, 1)

    twins = []

    def to_sibling(k):
        ref = grad.at[2 * chip(k) + q]
        twins.append(remote(ref, ref, sibling))

    all_gather(grad, lambda k: 2 * chip(k) + q, to_sibling)

    for copy in panel_copies:
        copy.wait_recv()
    panel = panels[owner_ref[0]]
    rows = NB * NY
    same_y = indicator((rows, rows), lambda r: r & (NY - 1), lambda c: c & (NY - 1))
    column = lax.rem(orb, 8) * NB
    of_column = jnp.where(indicator((rows, 128), lambda r: r // NY + column, lambda c: c), 1.0, 0.0)
    by_row = lax.dot_general(
        of_column, panel, (((1,), (1,)), ((), ())), preferred_element_type=F32,
        precision=lax.Precision.HIGHEST,
    )
    to_rows = jnp.where(indicator((NB, rows), lambda r: r, lambda c: c // NY), 1.0, 0.0)
    w_high, w_low = split(jnp.where(same_y, exact_dot(by_row, to_rows), 0.0))
    w_both = jnp.concatenate([w_high, w_low], 0)
    for copy in twins:
        copy.wait_recv()
    out_grad = pltpu.make_async_copy(grad, grad_hbm, loc.at[3])
    out_grad.start()
    outs = []
    for x in range(0, NX, 2):
        g_pair = jnp.concatenate([grad[:, x].reshape(rows, NZ), grad[:, x + 1].reshape(rows, NZ)], 1)
        g_high, g_low = split(g_pair)
        both = dot_nn(w_both, g_high)
        part = both[:rows] + both[rows:] + dot_nn(w_high, g_low)
        upd[:, x] = x2[q, :, x] + part[:, :NZ].reshape(NB, NY, NZ)
        upd[:, x + 1] = x2[q, :, x + 1] + part[:, NZ:].reshape(NB, NY, NZ)
        pair = pl.ds(x, 2)
        copy = pltpu.make_async_copy(upd.at[:, pair], upd_hbm.at[:, pair], loc.at[4 + x // 2])
        copy.start()
        outs.append(copy)
    for copy in started:
        copy.wait_send()
    out_grad.wait()
    for copy in outs:
        copy.wait()


def per_device(orbitals, potential, rotation, block, owner):
    shard = (NX, NY, NZ)
    half = (NX // 2, NY, NZ)
    scratch = [
        pltpu.VMEM((2, NB, *shard), F32),
        pltpu.VMEM((2, NB, *shard), BF),
        pltpu.VMEM((2, NB, *shard), BF),
        pltpu.VMEM(shard, F32),
        pltpu.VMEM((NB, NB * NORB), F32),
        pltpu.VMEM((NCHIP, *shard), F32),
        pltpu.VMEM((NCHIP, *shard), F32),
        pltpu.VMEM((NX + 2 * HALO, NY, NZ), F32),
        pltpu.VMEM(shard, F32),
        pltpu.VMEM((NCHIP, *shard), F32),
        pltpu.VMEM((NB, *shard), F32),
        pltpu.VMEM((NB, *shard), F32),
        pltpu.VMEM((NDOM, NCHIP, 128), F32),
        pltpu.VMEM((NORB, NB, 128), F32),
        pltpu.VMEM((2, 2, *shard), F32),
        pltpu.VMEM((2, 2, *half), F32),
        pltpu.VMEM((2, 2, *shard), F32),
        pltpu.VMEM((2, 2, *shard), F32),
        pltpu.VMEM((2, 2, *shard), F32),
        pltpu.SemaphoreType.DMA((112,)),
        pltpu.SemaphoreType.DMA((112,)),
        pltpu.SemaphoreType.DMA((8,)),
    ]
    smem = pl.BlockSpec(memory_space=pltpu.SMEM)
    hbm = pl.BlockSpec(memory_space=pl.ANY)
    return pl.pallas_call(
        kernel,
        out_shape=(
            jax.ShapeDtypeStruct((NB, *shard), F32),
            jax.ShapeDtypeStruct((NB, *shard), F32),
        ),
        in_specs=[smem, smem, hbm, hbm, hbm],
        out_specs=(hbm, hbm),
        scratch_shapes=scratch,
        compiler_params=pltpu.CompilerParams(
            collective_id=0, has_side_effects=True, vmem_limit_bytes=48 << 20
        ),
        cost_estimate=pl.CostEstimate(flops=1 << 28, bytes_accessed=3 << 20, transcendentals=0),
        name="gradient_update",
    )(block, owner, orbitals, potential, rotation)


def solution(mesh):
    in_specs = (P("orb", "dom", None, None), P("dom", None, None), P("orb", None), P(), P())
    out_specs = (P(None, "dom", None, None), P("orb", "dom", None, None))
    return jax.shard_map(
        per_device, mesh=mesh, in_specs=in_specs, out_specs=out_specs, check_vma=False
    )
```

time: 348 us -> 73.2 us (0.21)
  waiting for transfers between devices: 178 us -> 0 us
  blocking collectives: 81.3 us -> 0 us
  Pallas kernels: 0 us -> 66.3 us
  local copies, waits for them, and re-layouts: 38.6 us -> 4.72 us
  other arithmetic: 21.8 us -> 0 us
  between operations: 15.5 us -> 1.94 us
  matrix products: 7.46 us -> 0 us
  starting transfers between devices: 5.02 us -> 0 us
    psum x2 -> x0, waiting for transfers between devices: 178 us -> none  [the longest x1 115 us: from_root(): return lax.psum(jnp.where(mine, value, jnp.zeros_like(value)), axis)]
    psum x2 -> x0, blocking collectives: 81.3 us -> none  [the longest x1 51 us: from_root(): return lax.psum(jnp.where(mine, value, jnp.zeros_like(value)), axis)]
    pallas_call x0 -> x1, Pallas kernels: none -> 66.3 us  [per_device(): pl.pallas_call(kernel, out_shape=(jax.ShapeDtypeStruct((NB, *shard), F32)...]
    slice x25 -> x0, local copies, waits for them, and re-layouts: 34.5 us -> none  [the longest x24 32.9 us: hamiltonian(): jnp.roll(field, -offset, axis_pos)]
    add x1 -> x0, other arithmetic: 17.6 us -> none  [hamiltonian(): return -0.5 * summed + potential[None] * field]
    dot_general x3 -> x0, matrix products: 7.46 us -> none  [the longest x1 3.4 us: per_device(): jnp.einsum('axyz,cxyz->ac', orbitals, applied, precision=lax.Precision.HI...]
    ppermute x2 -> x0, starting transfers between devices: 4.94 us -> none  [the longest x1 3.65 us: padded_2(): after = lax.ppermute(leading, axis, down)]
  transfers between devices with their start and end apart: 4 -> 0, of which waited for: 2 -> 0; matrix products, arithmetic and copies ran while one was open for 10% -> 0% of each run, Pallas kernels for 0% -> 0%
where the time goes in v1:
time: 73.2 us; the launch traced here: 73 us
  Pallas kernels  66.3 us (91%)
  local copies, waits for them, and re-layouts  4.72 us (6%)
  between operations  1.94 us (3%)
    pallas_call x1, Pallas kernels, per_device(): pl.pallas_call(kernel, out_shape=(jax.ShapeDtypeStruct((NB, *shard), F32)...  66.3 us
    unnamed x8, local copies, waits for them, and re-layouts  4.72 us

profile of v1, /device:TPU:1, one launch (start us, length us, event | category | flops | bytes accessed | tf_op | source)
XLA Modules:
  0.0 73.0 jit_solution(4359175296616513072)
XLA Ops:
  1.9 0.0 copy-start
  1.9 1.2 %copy-done = f32[16,8,16,128]{3,2,1,0:T(8,128)S(1)} copy-done((f32[16,8,16,128]{3,2,1,0:T(8,128)S(1)}, f32[16,8,16,128]{3,2,1,0:T(8,128)}, u32[]{:S(2)}) %copy-start) | copy-done | bytes 1048600
  3.1 0.0 copy-start.1
  3.1 0.8 %copy-done.1 = f32[8,16,128]{2,1,0:T(8,128)S(1)} copy-done((f32[8,16,128]{2,1,0:T(8,128)S(1)}, f32[8,16,128]{2,1,0:T(8,128)}, u32[]{:S(2)}) %copy-start.1) | copy-done | bytes 65560
  4.0 0.0 copy-start.2
  4.0 0.7 copy-done.2
  4.7 66.3 %gradient_update.1 = (f32[16,8,16,128]{3,2,1,0:T(8,128)S(1)}, f32[16,8,16,128]{3,2,1,0:T(8,128)S(1)}) custom-call(s32[1]{0:T(128)S(6)} %copy.9.block_ref, s32[1]{0:T(128)S(6)} %copy.10.owner_ref, f32[16,8,16,128]{3,2,1,0:T(8,128)S(1)} %copy-done, f32[8,16,128]{2,1,0:T(8,128)S(1)} %copy-done.1, f32[16,256]{1,0:T(8,128)S(1)} %copy-done.2), custom_call_target="tpu_custom_call" | custom-call | flops 268435456 | bytes 3145728 | tf_op jit(solution)/shard_map/gradient_update/pallas_call | solution.py:329
  71.0 1.0 %copy.11 = f32[16,8,16,128]{3,2,1,0:T(8,128)} copy(f32[16,8,16,128]{3,2,1,0:T(8,128)S(1)} %get-tuple-element.4) | data formatting | bytes 2097152
  72.0 1.0 %copy.12 = f32[16,8,16,128]{3,2,1,0:T(8,128)} copy(f32[16,8,16,128]{3,2,1,0:T(8,128)S(1)} %get-tuple-element.5) | data formatting | bytes 2097152
Async XLA Ops:
  1.9 1.2 %copy-start = (f32[16,8,16,128]{3,2,1,0:T(8,128)S(1)}, f32[16,8,16,128]{3,2,1,0:T(8,128)}, u32[]{:S(2)}) copy-start(f32[16,8,16,128]{3,2,1,0:T(8,128)} %x_hbm.1) | copy-start | bytes 3145732
  3.1 0.8 %copy-start.1 = (f32[8,16,128]{2,1,0:T(8,128)S(1)}, f32[8,16,128]{2,1,0:T(8,128)}, u32[]{:S(2)}) copy-start(f32[8,16,128]{2,1,0:T(8,128)} %pot_hbm.1) | copy-start | bytes 196612
  4.0 0.7 copy-start.2

commit v2 on v1

v2 whole, which is shorter than its diff:
```python
import functools

import jax
import jax.numpy as jnp
from jax import lax
from jax.experimental import pallas as pl
from jax.experimental.pallas import tpu as pltpu
from jax.sharding import PartitionSpec as P

CENTER = -5369.0 / 1800.0
SIDES = (12.0 / 7.0, -15.0 / 56.0, 10.0 / 189.0, -1.0 / 112.0, 2.0 / 1925.0, -1.0 / 16632.0)

MESH = pl.DeviceIdType.MESH
NB = 16
NX, NY, NZ = 8, 16, 128
NDOM, NORB, NCHIP = 16, 16, 8
HALO = 6
BF = jnp.bfloat16
F32 = jnp.float32


def split(value):
    high = value.astype(BF)
    return high, (value - high.astype(F32)).astype(BF)


def dot_nt(a, b):
    return lax.dot_general(a, b, (((1,), (1,)), ((), ())), preferred_element_type=F32)


def dot_nn(a, b):
    return lax.dot_general(a, b, (((1,), (0,)), ((), ())), preferred_element_type=F32)


def indicator(shape, row_of, col_of):
    rows = lax.broadcasted_iota(jnp.int32, shape, 0)
    cols = lax.broadcasted_iota(jnp.int32, shape, 1)
    return row_of(rows) == col_of(cols)


def kernel(
    block_ref, owner_ref, x_hbm, pot_hbm, rot_hbm, grad_hbm, upd_hbm,
    x2, xh, xl, pot, rot, mask, remo, act, amat, grad, upd, pbuf, packed, panels,
    a1, a2, d1, b2, sb, send, recv, loc,
):
    dom = lax.axis_index("dom")
    orb = lax.axis_index("orb")
    z = lax.div(orb, 2)
    q = lax.rem(orb, 2)

    def chip(k):
        return lax.rem(z + (k + 2 * NCHIP), NCHIP)

    def peer(k):
        return (dom, 2 * chip(k) + q)

    def side(k):
        return (lax.rem(dom + (k + NDOM), NDOM), orb)

    sibling = (dom, orb + 1 - 2 * q)
    sems = iter(range(send.shape[0]))
    started = []

    def remote(src, dst, device):
        i = next(sems)
        copy = pltpu.make_async_remote_copy(
            src_ref=src, dst_ref=dst, send_sem=send.at[i], recv_sem=recv.at[i],
            device_id=device, device_id_type=MESH,
        )
        copy.start()
        started.append(copy)
        return copy

    def arrive(copies):
        for copy in copies:
            copy.wait_recv()

    load_x = pltpu.make_async_copy(x_hbm, x2.at[q], loc.at[0])
    load_pot = pltpu.make_async_copy(pot_hbm, pot, loc.at[1])
    load_rot = pltpu.make_async_copy(rot_hbm, rot, loc.at[2])
    for copy in (load_x, load_pot, load_rot):
        copy.start()
    barrier = pltpu.get_barrier_semaphore()
    for k in range(1, NDOM):
        pl.semaphore_signal(barrier, inc=1, device_id=side(k), device_id_type=MESH)
    for k in range(1, NORB):
        pl.semaphore_signal(
            barrier, inc=1, device_id=(dom, lax.rem(orb + k, NORB)), device_id_type=MESH
        )
    for copy in (load_x, load_pot, load_rot):
        copy.wait()
    pl.semaphore_wait(barrier, NDOM + NORB - 2)

    def scatter_far(part, slot, h):
        whole, front, back = pl.ds(4 * h, 4), pl.ds(4 * h, 2), pl.ds(4 * h + 2, 2)
        return (
            remote(part(4).at[front], a2.at[slot, 0, front], peer(2)),
            remote(part(4).at[back], a2.at[slot, 1, back], peer(-2)),
            remote(part(3).at[whole], a1.at[slot, 0, whole], peer(1)),
            remote(part(-3).at[whole], a1.at[slot, 1, whole], peer(-1)),
        )

    def scatter_mid(part, slot, h, far):
        whole, front, back = pl.ds(4 * h, 4), pl.ds(4 * h, 2), pl.ds(4 * h + 2, 2)
        sent = []
        for i, sign, quarter in ((0, 1, front), (1, -1, back)):
            arrive((far[i], far[2 + i]))
            sb[slot, i, whole] = part(2 * sign)[whole] + a1[slot, i, whole]
            sb[slot, i, quarter] = sb[slot, i, quarter] + a2[slot, i, quarter]
            sent.append(remote(sb.at[slot, i, whole], b2.at[slot, i, whole], peer(2 * sign)))
        return tuple(sent)

    def scatter_near(part, slot, h):
        whole = pl.ds(4 * h, 4)
        return (
            remote(part(1).at[whole], d1.at[slot, 0, whole], peer(1)),
            remote(part(-1).at[whole], d1.at[slot, 1, whole], peer(-1)),
        )

    def scatter_sum(part, slot, h, copies):
        whole = pl.ds(4 * h, 4)
        arrive(copies)
        return (
            part(0)[whole]
            + (d1[slot, 0, whole] + d1[slot, 1, whole])
            + (b2[slot, 0, whole] + b2[slot, 1, whole])
        )

    def give(shard, k, to, planes):
        ref = shard(k).at[planes]
        return remote(ref, ref, peer(to))

    def gather_two(shard, h):
        whole = pl.ds(4 * h, 4)
        return give(shard, 0, 2, whole), give(shard, 0, -2, whole)

    def gather_one(shard, h):
        whole = pl.ds(4 * h, 4)
        return give(shard, 0, 1, whole), give(shard, 0, -1, whole)

    def gather_on(shard, h, two, arrived=lambda k, h: None):
        whole, front, back = pl.ds(4 * h, 4), pl.ds(4 * h, 2), pl.ds(4 * h + 2, 2)
        arrive(two[:1])
        ahead = give(shard, -2, 2, front), give(shard, -2, 1, whole)
        arrived(-2, h)
        arrive(two[1:])
        behind = give(shard, 2, -2, back), give(shard, 2, -1, whole)
        arrived(2, h)
        return ahead + behind

    order = (4, 3, -3, 2, -2, 1, -1, 0)

    def to_twin(k, parity):
        ref = x2.at[q, 2 * chip(k) + parity]
        return remote(ref, ref, sibling)

    wanted = [to_twin(k, 1 - q) for k in order]
    others = [to_twin(k, q) for k in order]

    block = block_ref[0]
    root_core = lax.rem(block, 2)
    is_root = lax.div(block, 2) == z

    def masked(k):
        return mask.at[chip(k)]

    def fill(pairs):
        for k, copy in pairs:
            copy.wait_recv()
            i = 2 * chip(k) + q
            mine = jnp.where(root_core == 0, x2[0, i], x2[1, i])
            mask[chip(k)] = jnp.where(is_root, mine, 0.0)

    pairs = list(zip(order, wanted))
    fill(pairs[:3])
    far = [scatter_far(masked, 0, h) for h in range(2)]
    fill(pairs[3:])
    near = [scatter_near(masked, 0, h) for h in range(2)]
    mid = [scatter_mid(masked, 0, h, far[h]) for h in range(2)]
    for h in range(2):
        act[pl.ds(HALO + 4 * h, 4)] = scatter_sum(masked, 0, h, near[h] + mid[h])

    halo = (
        remote(act.at[pl.ds(NX, HALO)], act.at[pl.ds(0, HALO)], side(1)),
        remote(act.at[pl.ds(HALO, HALO)], act.at[pl.ds(HALO + NX, HALO)], side(-1)),
    )

    r_high, r_low = split(rot[...])
    r_both = jnp.concatenate([r_high, r_low], 0)
    for j in range(0, NORB, 2):
        base = (j // 8) * 128
        shape = (128, 256)
        pick = indicator(
            shape, lambda r: r + base, lambda c: (j + (c >> 7)) * NB + (c & (NB - 1))
        )
        both = dot_nn(r_both[:, base : base + 128], jnp.where(pick, 1.0, 0.0).astype(BF))
        both = both[:NB] + both[NB:]
        own = indicator((NB, 256), lambda r: r & 7, lambda c: (c & 127) >> 4)
        both = jnp.where(own, both, 0.0).reshape(2, 8, 256).sum(1)
        packed[j] = both[:, :128]
        packed[j + 1] = both[:, 128:]
    panels[orb] = packed[orb]
    panel_copies = []
    for k in range(1, NORB):
        to = lax.rem(orb + k, NORB)
        panel_copies.append(remote(packed.at[to], panels.at[orb], (dom, to)))

    field = act[pl.ds(HALO, NX)]
    inner = (pot[...] - 1.5 * CENTER) * field
    for k in range(1, 7):
        near = (
            pltpu.roll(field, k, 1) + pltpu.roll(field, NY - k, 1)
            + pltpu.roll(field, k, 2) + pltpu.roll(field, NZ - k, 2)
        )
        inner = inner - (0.5 * SIDES[k - 1]) * near
    arrive(others)
    for j in range(2):
        def cast(a, carry, j=j):
            high, low = split(x2[j, a])
            xh[j, a] = high
            xl[j, a] = low
            return carry
        lax.fori_loop(0, NB, cast, 0)
    arrive(halo)
    for k in range(1, 7):
        inner = inner - (0.5 * SIDES[k - 1]) * (act[pl.ds(HALO + k, NX)] + act[pl.ds(HALO - k, NX)])
    amat[z] = inner

    cols = 2 * NB * NY

    def shard(k):
        return amat.at[chip(k)]

    def same_y(rows):
        return indicator((rows, cols), lambda r: r & (NY - 1), lambda c: c & (NY - 1))

    def x_pairs():
        for x in range(0, NX, 2):
            yield x, *(
                jnp.concatenate([r[:, :, x].reshape(cols, NZ), r[:, :, x + 1].reshape(cols, NZ)], 1)
                for r in (xh, xl)
            )

    def project(batch, ks):
        rows = len(ks) * NY
        gram = jnp.zeros((rows, cols), F32)
        for x, h_pair, l_pair in x_pairs():
            a_pair = jnp.concatenate([
                jnp.concatenate([shard(k)[x] for k in ks], 0),
                jnp.concatenate([shard(k)[x + 1] for k in ks], 0),
            ], 1)
            a_high, a_low = split(a_pair)
            both = dot_nt(jnp.concatenate([a_high, a_low], 0), h_pair)
            gram = gram + (both[:rows] + both[rows:] + dot_nt(a_high, l_pair))
        summed = jnp.where(same_y(rows), gram, 0.0).reshape(len(ks), NY, cols).sum(1)
        summed = jnp.concatenate([summed, jnp.zeros((8 - len(ks), cols), F32)], 0)
        of_orbital = indicator((cols, 128), lambda r: r >> 4, lambda c: c)
        s_both = jnp.concatenate(split(summed), 0)
        summed = dot_nn(s_both, jnp.where(of_orbital, 1.0, 0.0).astype(BF))
        pbuf[batch, dom] = summed[:8] + summed[8:]
        ref = pbuf.at[batch, dom]
        return [remote(ref, ref, side(k)) for k in range(1, NDOM)]

    def remove(batch, ks, copies, halves):
        rows = len(ks) * NY
        arrive(copies)
        proj = pbuf[batch].sum(0) * (1.0 / (NX * NDOM * NY * NZ))
        to_rows = indicator((128, cols), lambda r: r, lambda c: c >> 4)
        spread = dot_nn(
            jnp.concatenate(split(proj), 0), jnp.where(to_rows, 1.0, 0.0).astype(BF)
        )
        keep = same_y(rows)
        weights = []
        for first in (0, 8):
            one = spread[first : first + len(ks)]
            one = jnp.broadcast_to(one[:, None, :], (len(ks), NY, cols)).reshape(rows, cols)
            weights.append(jnp.where(keep, one, 0.0).astype(BF))
        k_both = jnp.concatenate(weights, 0)
        for x, h_pair, l_pair in x_pairs():
            both = dot_nn(k_both, h_pair)
            part = both[:rows] + both[rows:] + dot_nn(weights[0], l_pair)
            for i, k in enumerate(ks):
                remo[chip(k), x] = part[i * NY : (i + 1) * NY, :NZ]
                remo[chip(k), x + 1] = part[i * NY : (i + 1) * NY, NZ:]
            if x == 2 or x == 6:
                halves(x // 4)

    two = [gather_two(shard, 0)]
    one = [gather_one(shard, 0), gather_one(shard, 1)]
    two.append(gather_two(shard, 1))
    on = [gather_on(shard, 0, two[0])]
    arrive(one[0] + one[1])
    batches = ((0, 1, -1), (2, -2), (3, -3, 4))
    sums = [project(0, batches[0])]
    on.append(gather_on(shard, 1, two[1]))
    sums.append(project(1, batches[1]))

    def removed(k):
        return remo.at[chip(k + 4)]

    def owned(k):
        return grad.at[2 * chip(k + 4) + q]

    far, mid, near, twins = [], [], [], [[], []]
    remove(0, batches[0], sums[0], lambda h: far.append(scatter_far(removed, 1, h)))
    arrive(on[0] + on[1])
    sums.append(project(2, batches[2]))
    remove(1, batches[1], sums[1], lambda h: None)
    mid.append(scatter_mid(removed, 1, 0, far[0]))
    mid.append(scatter_mid(removed, 1, 1, far[1]))
    remove(2, batches[2], sums[2], lambda h: near.append(scatter_near(removed, 1, h)))

    def to_sibling(k, h):
        ref = owned(k).at[pl.ds(4 * h, 4)]
        twins[h].append(remote(ref, ref, sibling))

    two, one, on = [], [], []
    for h in range(2):
        half = pl.ds(4 * h, 4)
        owned(0)[half] = amat[chip(4), half] - scatter_sum(removed, 1, h, near[h] + mid[h])
        two.append(gather_two(owned, h))
        one.append(gather_one(owned, h))
        to_sibling(0, h)

    arrive(panel_copies)
    rows = NB * NY
    panel = panels[owner_ref[0]]
    panel = jnp.broadcast_to(panel[:, None, :], (2, 8, 128)).reshape(NB, 128)
    own = indicator((NB, 128), lambda r: r & 7, lambda c: c >> 4)
    p_both = jnp.concatenate(split(jnp.where(own, panel, 0.0)), 0)
    of_column = indicator((rows, 128), lambda r: r >> 4, lambda c: c & (NB - 1))
    by_row = dot_nt(jnp.where(of_column, 1.0, 0.0).astype(BF), p_both).astype(BF)
    to_rows = indicator((NB, rows), lambda r: r, lambda c: c >> 4)
    to_rows = jnp.where(to_rows, 1.0, 0.0).astype(BF)
    keep = indicator((rows, rows), lambda r: r & (NY - 1), lambda c: c & (NY - 1))
    w_high, w_low = (
        jnp.where(keep, dot_nn(one_of, to_rows), 0.0).astype(BF)
        for one_of in (by_row[:, :NB], by_row[:, NB:])
    )
    w_both = jnp.concatenate([w_high, w_low], 0)

    for h in range(2):
        on.append(gather_on(owned, h, two[h], to_sibling))
    for h in range(2):
        for i, k in ((0, -1), (1, 1)):
            arrive(one[h][i : i + 1])
            to_sibling(k, h)
    outs = []
    for h in range(2):
        arrive(on[h][1:2])
        to_sibling(-3, h)
        arrive(on[h][3:4])
        to_sibling(3, h)
        arrive((on[h][0], on[h][2]))
        to_sibling(4, h)
        arrive(twins[h])
        half = pl.ds(4 * h, 4)
        outs.append(pltpu.make_async_copy(grad.at[:, half], grad_hbm.at[:, half], loc.at[3 + h]))
        outs[-1].start()
        for x in range(4 * h, 4 * h + 4, 2):
            g_pair = jnp.concatenate(
                [grad[:, x].reshape(rows, NZ), grad[:, x + 1].reshape(rows, NZ)], 1
            )
            g_high, g_low = split(g_pair)
            both = dot_nn(w_both, g_high)
            part = both[:rows] + both[rows:] + dot_nn(w_high, g_low)
            upd[:, x] = x2[q, :, x] + part[:, :NZ].reshape(NB, NY, NZ)
            upd[:, x + 1] = x2[q, :, x + 1] + part[:, NZ:].reshape(NB, NY, NZ)
        outs.append(pltpu.make_async_copy(upd.at[:, half], upd_hbm.at[:, half], loc.at[5 + h]))
        outs[-1].start()
    for copy in started:
        copy.wait_send()
    for copy in outs:
        copy.wait()


def per_device(orbitals, potential, rotation, block, owner):
    shard = (NX, NY, NZ)
    scratch = [
        pltpu.VMEM((2, NB, *shard), F32),
        pltpu.VMEM((2, NB, *shard), BF),
        pltpu.VMEM((2, NB, *shard), BF),
        pltpu.VMEM(shard, F32),
        pltpu.VMEM((NB, NB * NORB), F32),
        pltpu.VMEM((NCHIP, *shard), F32),
        pltpu.VMEM((NCHIP, *shard), F32),
        pltpu.VMEM((NX + 2 * HALO, NY, NZ), F32),
        pltpu.VMEM((NCHIP, *shard), F32),
        pltpu.VMEM((NB, *shard), F32),
        pltpu.VMEM((NB, *shard), F32),
        pltpu.VMEM((3, NDOM, 8, 128), F32),
        pltpu.VMEM((NORB, 2, 128), F32),
        pltpu.VMEM((NORB, 2, 128), F32),
        pltpu.VMEM((2, 2, *shard), F32),
        pltpu.VMEM((2, 2, *shard), F32),
        pltpu.VMEM((2, 2, *shard), F32),
        pltpu.VMEM((2, 2, *shard), F32),
        pltpu.VMEM((2, 2, *shard), F32),
        pltpu.SemaphoreType.DMA((160,)),
        pltpu.SemaphoreType.DMA((160,)),
        pltpu.SemaphoreType.DMA((8,)),
    ]
    smem = pl.BlockSpec(memory_space=pltpu.SMEM)
    hbm = pl.BlockSpec(memory_space=pl.ANY)
    return pl.pallas_call(
        kernel,
        out_shape=(
            jax.ShapeDtypeStruct((NB, *shard), F32),
            jax.ShapeDtypeStruct((NB, *shard), F32),
        ),
        in_specs=[smem, smem, hbm, hbm, hbm],
        out_specs=(hbm, hbm),
        scratch_shapes=scratch,
        compiler_params=pltpu.CompilerParams(
            collective_id=0, has_side_effects=True, vmem_limit_bytes=48 << 20
        ),
        cost_estimate=pl.CostEstimate(flops=1 << 28, bytes_accessed=3 << 20, transcendentals=0),
        name="gradient_update",
    )(
        block, owner,
        *(pltpu.with_memory_space_constraint(v, pltpu.HBM) for v in (orbitals, potential, rotation)),
    )


def solution(mesh):
    in_specs = (P("orb", "dom", None, None), P("dom", None, None), P("orb", None), P(), P())
    out_specs = (P(None, "dom", None, None), P("orb", "dom", None, None))
    return jax.shard_map(
        per_device, mesh=mesh, in_specs=in_specs, out_specs=out_specs, check_vma=False
    )
```

time: 73.2 us -> 66.8 us (0.913)
  Pallas kernels: 66.3 us -> 62.8 us
  local copies, waits for them, and re-layouts: 4.72 us -> 1.94 us
    pallas_call x1, Pallas kernels: 66.3 us -> 62.8 us  [per_device(): pl.pallas_call(kernel, out_shape=(jax.ShapeDtypeStruct((NB, *shard), F32)...]
    unnamed x8 -> x2, local copies, waits for them, and re-layouts: 4.72 us -> 1.94 us
where the time goes in v2:
time: 66.8 us; the launch traced here: 66.7 us
  Pallas kernels  62.8 us (94%)
  local copies, waits for them, and re-layouts  1.94 us (3%)
  between operations  1.93 us (3%)
    pallas_call x1, Pallas kernels, per_device(): pl.pallas_call(kernel, out_shape=(jax.ShapeDtypeStruct((NB, *shard), F32)...  62.8 us
    unnamed x2, local copies, waits for them, and re-layouts  1.94 us

profile of v2, /device:TPU:1, one launch (start us, length us, event | category | flops | bytes accessed | tf_op | source)
XLA Modules:
  0.0 66.7 jit_solution(12807913449795988338)
XLA Ops:
  1.9 62.8 %gradient_update.1 = (f32[16,8,16,128]{3,2,1,0:T(8,128)S(1)}, f32[16,8,16,128]{3,2,1,0:T(8,128)S(1)}) custom-call(s32[1]{0:T(128)S(6)} %copy.9.block_ref, s32[1]{0:T(128)S(6)} %copy.10.owner_ref, f32[16,8,16,128]{3,2,1,0:T(8,128)} %x_hbm.1, f32[8,16,128]{2,1,0:T(8,128)} %pot_hbm.1, f32[16,256]{1,0:T(8,128)} %rot_hbm.1), custom_call_target="tpu_custom_call" | custom-call | flops 268435456 | bytes 3145728 | tf_op jit(solution)/shard_map/gradient_update/pallas_call | solution.py:405
  64.7 1.0 %copy.11 = f32[16,8,16,128]{3,2,1,0:T(8,128)} copy(f32[16,8,16,128]{3,2,1,0:T(8,128)S(1)} %get-tuple-element.4) | data formatting | bytes 2097152
  65.7 1.0 %copy.12 = f32[16,8,16,128]{3,2,1,0:T(8,128)} copy(f32[16,8,16,128]{3,2,1,0:T(8,128)S(1)} %get-tuple-element.5) | data formatting | bytes 2097152

commit v3 on v2

--- a/solution.py
+++ b/solution.py
@@ -39,8 +39,8 @@
 
 
 def kernel(
-    block_ref, owner_ref, x_hbm, pot_hbm, rot_hbm, grad_hbm, upd_hbm,
-    x2, xh, xl, pot, rot, mask, remo, act, amat, grad, upd, pbuf, packed, panels,
+    block_ref, owner_ref, x_hbm, pot_hbm, rot_hbm, grad, w_ref, upd,
+    x2, xh, xl, pot, rot, mask, remo, act, amat, pbuf, packed, panels,
     a1, a2, d1, b2, sb, send, recv, loc,
 ):
     dom = lax.axis_index("dom")
@@ -75,19 +75,21 @@
         for copy in copies:
             copy.wait_recv()
 
-    load_x = pltpu.make_async_copy(x_hbm, x2.at[q], loc.at[0])
-    load_pot = pltpu.make_async_copy(pot_hbm, pot, loc.at[1])
-    load_rot = pltpu.make_async_copy(rot_hbm, rot, loc.at[2])
-    for copy in (load_x, load_pot, load_rot):
-        copy.start()
+    loads = [
+        pltpu.make_async_copy(src, dst, loc.at[i])
+        for i, (src, dst) in enumerate(((x_hbm, x2.at[q]), (pot_hbm, pot), (rot_hbm, rot)))
+    ]
+    loads[0].start()
     barrier = pltpu.get_barrier_semaphore()
+    for k in (8, 9, 7, 10, 6, 11, 5, 12, 4, 13, 3, 14, 2, 15, 1):
+        pl.semaphore_signal(
+            barrier, inc=1, device_id=(dom, lax.rem(orb + k, NORB)), device_id_type=MESH
+        )
     for k in range(1, NDOM):
         pl.semaphore_signal(barrier, inc=1, device_id=side(k), device_id_type=MESH)
-    for k in range(1, NORB):
-        pl.semaphore_signal(
-            barrier, inc=1, device_id=(dom, lax.rem(orb + k, NORB)), device_id_type=MESH
-        )
-    for copy in (load_x, load_pot, load_rot):
+    for copy in loads[1:]:
+        copy.start()
+    for copy in loads:
         copy.wait()
     pl.semaphore_wait(barrier, NDOM + NORB - 2)
 
@@ -155,7 +157,6 @@
         return remote(ref, ref, sibling)
 
     wanted = [to_twin(k, 1 - q) for k in order]
-    others = [to_twin(k, q) for k in order]
 
     block = block_ref[0]
     root_core = lax.rem(block, 2)
@@ -176,14 +177,20 @@
     far = [scatter_far(masked, 0, h) for h in range(2)]
     fill(pairs[3:])
     near = [scatter_near(masked, 0, h) for h in range(2)]
+    others = [to_twin(k, q) for k in order]
     mid = [scatter_mid(masked, 0, h, far[h]) for h in range(2)]
-    for h in range(2):
-        act[pl.ds(HALO + 4 * h, 4)] = scatter_sum(masked, 0, h, near[h] + mid[h])
-
-    halo = (
-        remote(act.at[pl.ds(NX, HALO)], act.at[pl.ds(0, HALO)], side(1)),
-        remote(act.at[pl.ds(HALO, HALO)], act.at[pl.ds(HALO + NX, HALO)], side(-1)),
-    )
+
+    halo = []
+
+    def lend(first, planes, to, shift):
+        halo.append(remote(act.at[pl.ds(first, planes)], act.at[pl.ds(first + shift, planes)], side(to)))
+
+    act[pl.ds(HALO, 4)] = scatter_sum(masked, 0, 0, near[0] + mid[0])
+    lend(HALO, 4, -1, NX)
+    lend(HALO + 2, 2, 1, -NX)
+    act[pl.ds(HALO + 4, 4)] = scatter_sum(masked, 0, 1, near[1] + mid[1])
+    lend(HALO + 4, 2, -1, NX)
+    lend(HALO + 4, 4, 1, -NX)
 
     r_high, r_low = split(rot[...])
     r_both = jnp.concatenate([r_high, r_low], 0)
@@ -253,11 +260,11 @@
             both = dot_nt(jnp.concatenate([a_high, a_low], 0), h_pair)
             gram = gram + (both[:rows] + both[rows:] + dot_nt(a_high, l_pair))
         summed = jnp.where(same_y(rows), gram, 0.0).reshape(len(ks), NY, cols).sum(1)
-        summed = jnp.concatenate([summed, jnp.zeros((8 - len(ks), cols), F32)], 0)
+        summed = jnp.concatenate([summed, jnp.zeros((4 - len(ks), cols), F32)], 0)
         of_orbital = indicator((cols, 128), lambda r: r >> 4, lambda c: c)
         s_both = jnp.concatenate(split(summed), 0)
         summed = dot_nn(s_both, jnp.where(of_orbital, 1.0, 0.0).astype(BF))
-        pbuf[batch, dom] = summed[:8] + summed[8:]
+        pbuf[batch, dom] = summed[:4] + summed[4:]
         ref = pbuf.at[batch, dom]
         return [remote(ref, ref, side(k)) for k in range(1, NDOM)]
 
@@ -271,7 +278,7 @@
         )
         keep = same_y(rows)
         weights = []
-        for first in (0, 8):
+        for first in (0, 4):
             one = spread[first : first + len(ks)]
             one = jnp.broadcast_to(one[:, None, :], (len(ks), NY, cols)).reshape(rows, cols)
             weights.append(jnp.where(keep, one, 0.0).astype(BF))
@@ -285,13 +292,12 @@
             if x == 2 or x == 6:
                 halves(x // 4)
 
-    two = [gather_two(shard, 0)]
     one = [gather_one(shard, 0), gather_one(shard, 1)]
-    two.append(gather_two(shard, 1))
-    on = [gather_on(shard, 0, two[0])]
+    two = [gather_two(shard, 0), gather_two(shard, 1)]
     arrive(one[0] + one[1])
     batches = ((0, 1, -1), (2, -2), (3, -3, 4))
     sums = [project(0, batches[0])]
+    on = [gather_on(shard, 0, two[0])]
     on.append(gather_on(shard, 1, two[1]))
     sums.append(project(1, batches[1]))
 
@@ -339,13 +345,15 @@
     )
     w_both = jnp.concatenate([w_high, w_low], 0)
 
+    w_ref[...] = w_both
+    upd[:, 4:] = x2[q, :, 4:]
+
     for h in range(2):
         on.append(gather_on(owned, h, two[h], to_sibling))
     for h in range(2):
         for i, k in ((0, -1), (1, 1)):
             arrive(one[h][i : i + 1])
             to_sibling(k, h)
-    outs = []
     for h in range(2):
         arrive(on[h][1:2])
         to_sibling(-3, h)
@@ -353,23 +361,39 @@
         to_sibling(3, h)
         arrive((on[h][0], on[h][2]))
         to_sibling(4, h)
-        arrive(twins[h])
-        half = pl.ds(4 * h, 4)
-        outs.append(pltpu.make_async_copy(grad.at[:, half], grad_hbm.at[:, half], loc.at[3 + h]))
-        outs[-1].start()
-        for x in range(4 * h, 4 * h + 4, 2):
-            g_pair = jnp.concatenate(
-                [grad[:, x].reshape(rows, NZ), grad[:, x + 1].reshape(rows, NZ)], 1
-            )
-            g_high, g_low = split(g_pair)
-            both = dot_nn(w_both, g_high)
-            part = both[:rows] + both[rows:] + dot_nn(w_high, g_low)
-            upd[:, x] = x2[q, :, x] + part[:, :NZ].reshape(NB, NY, NZ)
-            upd[:, x + 1] = x2[q, :, x + 1] + part[:, NZ:].reshape(NB, NY, NZ)
-        outs.append(pltpu.make_async_copy(upd.at[:, half], upd_hbm.at[:, half], loc.at[5 + h]))
-        outs[-1].start()
+
+    arrive(twins[0])
+    for x in range(0, 4, 2):
+        update(grad, w_both, x2.at[q], upd, x, x)
+    arrive(twins[1])
     for copy in started:
         copy.wait_send()
+
+
+def update(grad, w_both, old, new, x, at):
+    rows = NB * NY
+    g_pair = jnp.concatenate([grad[:, x].reshape(rows, NZ), grad[:, x + 1].reshape(rows, NZ)], 1)
+    g_high, g_low = split(g_pair)
+    both = dot_nn(w_both, g_high)
+    part = both[:rows] + both[rows:] + dot_nn(w_both[:rows], g_low)
+    new[:, at] = old[:, x] + part[:, :NZ].reshape(NB, NY, NZ)
+    new[:, at + 1] = old[:, x + 1] + part[:, NZ:].reshape(NB, NY, NZ)
+
+
+def update_kernel(grad, w_ref, upd, grad_hbm, upd_hbm, done, sem):
+    outs = []
+
+    def out(src, dst):
+        outs.append(pltpu.make_async_copy(src, dst, sem.at[len(outs)]))
+        outs[-1].start()
+
+    out(upd.at[:, pl.ds(0, 4)], upd_hbm.at[:, pl.ds(0, 4)])
+    out(grad, grad_hbm)
+    w_both = w_ref[...]
+    for x in range(4, NX, 2):
+        pair = pl.ds(x, 2)
+        update(grad, w_both, upd, done, x, x - 4)
+        out(done.at[:, pl.ds(x - 4, 2)], upd_hbm.at[:, pair])
     for copy in outs:
         copy.wait()
 
@@ -386,9 +410,7 @@
         pltpu.VMEM((NCHIP, *shard), F32),
         pltpu.VMEM((NX + 2 * HALO, NY, NZ), F32),
         pltpu.VMEM((NCHIP, *shard), F32),
-        pltpu.VMEM((NB, *shard), F32),
-        pltpu.VMEM((NB, *shard), F32),
-        pltpu.VMEM((3, NDOM, 8, 128), F32),
+        pltpu.VMEM((3, NDOM, 4, 128), F32),
         pltpu.VMEM((NORB, 2, 128), F32),
         pltpu.VMEM((NORB, 2, 128), F32),
         pltpu.VMEM((2, 2, *shard), F32),
@@ -400,26 +422,36 @@
         pltpu.SemaphoreType.DMA((160,)),
         pltpu.SemaphoreType.DMA((8,)),
     ]
+    hbm = pl.BlockSpec(memory_space=pl.ANY)
     smem = pl.BlockSpec(memory_space=pltpu.SMEM)
-    hbm = pl.BlockSpec(memory_space=pl.ANY)
-    return pl.pallas_call(
+    vmem = pl.BlockSpec(memory_space=pltpu.VMEM)
+    whole = jax.ShapeDtypeStruct((NB, *shard), F32)
+    arrays = (pltpu.with_memory_space_constraint(v, pltpu.HBM) for v in (orbitals, potential, rotation))
+    gradient, weights, updated = pl.pallas_call(
         kernel,
-        out_shape=(
-            jax.ShapeDtypeStruct((NB, *shard), F32),
-            jax.ShapeDtypeStruct((NB, *shard), F32),
-        ),
+        out_shape=(whole, jax.ShapeDtypeStruct((2 * NB * NY, NB * NY), BF), whole),
         in_specs=[smem, smem, hbm, hbm, hbm],
-        out_specs=(hbm, hbm),
+        out_specs=(vmem, vmem, vmem),
         scratch_shapes=scratch,
         compiler_params=pltpu.CompilerParams(
-            collective_id=0, has_side_effects=True, vmem_limit_bytes=48 << 20
+            collective_id=0, has_side_effects=True, vmem_limit_bytes=40 << 20
         ),
         cost_estimate=pl.CostEstimate(flops=1 << 28, bytes_accessed=3 << 20, transcendentals=0),
-        name="gradient_update",
-    )(
-        block, owner,
-        *(pltpu.with_memory_space_constraint(v, pltpu.HBM) for v in (orbitals, potential, rotation)),
-    )
+        name="gradient",
+    )(block, owner, *arrays)
+    return pl.pallas_call(
+        update_kernel,
+        out_shape=(whole, whole),
+        in_specs=[vmem, vmem, vmem],
+        out_specs=(hbm, hbm),
+        scratch_shapes=[
+            pltpu.VMEM((NB, NX // 2, NY, NZ), F32),
+            pltpu.SemaphoreType.DMA((4,)),
+        ],
+        compiler_params=pltpu.CompilerParams(vmem_limit_bytes=16 << 20),
+        cost_estimate=pl.CostEstimate(flops=1 << 28, bytes_accessed=4 << 20, transcendentals=0),
+        name="update",
+    )(gradient, weights, updated)
 
 
 def solution(mesh):

time: 66.8 us -> 64.2 us (0.961)
  local copies, waits for them, and re-layouts: 1.94 us -> 0 us
  Pallas kernels: 62.8 us -> 62.1 us
    unnamed x2 -> x0, local copies, waits for them, and re-layouts: 1.94 us -> none
    pallas_call x1 -> x2, Pallas kernels: 62.8 us -> 62.1 us  [the longest x1 60.8 us: per_device(): pl.pallas_call(kernel, out_shape=(whole, jax.ShapeDtypeStruct((2 * NB * N...]
where the time goes in v3:
time: 64.2 us; the launch traced here: 64.1 us
  Pallas kernels  62.1 us (97%)
  between operations  1.93 us (3%)
    pallas_call x1, Pallas kernels, per_device(): pl.pallas_call(kernel, out_shape=(whole, jax.ShapeDtypeStruct((2 * NB * N...  60.8 us
    pallas_call x1, Pallas kernels, per_device(): pl.pallas_call(update_kernel, out_shape=(whole, whole), in_specs=[vmem, v...  1.37 us

profile of v3, /device:TPU:1, one launch (start us, length us, event | category | flops | bytes accessed | tf_op | source)
XLA Modules:
  0.0 64.1 jit_solution(5020920721950392351)
XLA Ops:
  1.9 60.8 %gradient.1 = (f32[16,8,16,128]{3,2,1,0:T(8,128)S(1)}, bf16[512,256]{1,0:T(8,128)(2,1)S(1)}, f32[16,8,16,128]{3,2,1,0:T(8,128)S(1)}) custom-call(s32[1]{0:T(128)S(6)} %copy.7.block_ref, s32[1]{0:T(128)S(6)} %copy.8.owner_ref, f32[16,8,16,128]{3,2,1,0:T(8,128)} %x_hbm.1, f32[8,16,128]{2,1,0:T(8,128)} %pot_hbm.1, f32[16,256]{1,0:T(8,128)} %rot_hbm.1), custom_call_target="tpu_custom_call" | custom-call | flops 268435456 | bytes 3145728 | tf_op jit(solution)/shard_map/gradient/pallas_call | solution.py:430
  62.7 1.4 %update.1 = (f32[16,8,16,128]{3,2,1,0:T(8,128)}, f32[16,8,16,128]{3,2,1,0:T(8,128)}) custom-call(f32[16,8,16,128]{3,2,1,0:T(8,128)S(1)} %get-tuple-element.5.grad, bf16[512,256]{1,0:T(8,128)(2,1)S(1)} %get-tuple-element.6.w_ref, f32[16,8,16,128]{3,2,1,0:T(8,128)S(1)} %get-tuple-element.7.upd), custom_call_target="tpu_custom_call" | custom-call | flops 268435456 | bytes 4194304 | tf_op jit(solution)/shard_map/update/pallas_call | solution.py:442

commit v4 on v3

--- a/solution.py
+++ b/solution.py
@@ -1,4 +1,5 @@
-import functools
+import itertools
+import math
 
 import jax
 import jax.numpy as jnp
@@ -58,22 +59,39 @@
         return (lax.rem(dom + (k + NDOM), NDOM), orb)
 
     sibling = (dom, orb + 1 - 2 * q)
-    sems = iter(range(send.shape[0]))
-    started = []
-
-    def remote(src, dst, device):
-        i = next(sems)
-        copy = pltpu.make_async_remote_copy(
-            src_ref=src, dst_ref=dst, send_sem=send.at[i], recv_sem=recv.at[i],
+    groups = itertools.count()
+    sent = [dict(sem=i, rows=0) for i in range(send.shape[0])]
+    phase = [0]
+
+    def new(span=None):
+        return dict(sem=next(groups), rows=0, span=span)
+
+    def remote(src, dst, device, group, sends=None):
+        sends = sent[phase[0]] if sends is None else sends
+        pltpu.make_async_remote_copy(
+            src_ref=src, dst_ref=dst, send_sem=send.at[sends["sem"]], recv_sem=recv.at[group["sem"]],
             device_id=device, device_id_type=MESH,
+        ).start()
+        for one in (group, sends):
+            one["rows"] += math.prod(src.shape[:-1])
+
+    def span(group):
+        planes = group["rows"] // NY
+        if group.get("span") is not None:
+            ref = group["span"]
+        elif planes <= act.shape[0]:
+            ref = act.at[pl.ds(0, planes)]
+        else:
+            ref = x2.at[0, pl.ds(0, planes // NX)]
+        assert math.prod(ref.shape[:-1]) == group["rows"]
+        return pltpu.make_async_remote_copy(
+            src_ref=ref, dst_ref=ref, send_sem=send.at[group["sem"] % len(sent)],
+            recv_sem=recv.at[group["sem"]], device_id=sibling, device_id_type=MESH,
         )
-        copy.start()
-        started.append(copy)
-        return copy
-
-    def arrive(copies):
-        for copy in copies:
-            copy.wait_recv()
+
+    def arrive(*waited):
+        for group in waited:
+            span(group).wait_recv()
 
     loads = [
         pltpu.make_async_copy(src, dst, loc.at[i])
@@ -95,68 +113,72 @@
 
     def scatter_far(part, slot, h):
         whole, front, back = pl.ds(4 * h, 4), pl.ds(4 * h, 2), pl.ds(4 * h + 2, 2)
-        return (
-            remote(part(4).at[front], a2.at[slot, 0, front], peer(2)),
-            remote(part(4).at[back], a2.at[slot, 1, back], peer(-2)),
-            remote(part(3).at[whole], a1.at[slot, 0, whole], peer(1)),
-            remote(part(-3).at[whole], a1.at[slot, 1, whole], peer(-1)),
-        )
-
-    def scatter_mid(part, slot, h, far):
+        up, down = new(), new()
+        remote(part(4).at[front], a2.at[slot, 0, front], peer(2), up)
+        remote(part(4).at[back], a2.at[slot, 1, back], peer(-2), down)
+        remote(part(3).at[whole], a1.at[slot, 0, whole], peer(1), up)
+        remote(part(-3).at[whole], a1.at[slot, 1, whole], peer(-1), down)
+        return up, down
+
+    def scatter_mid(part, slot, h, far, last):
         whole, front, back = pl.ds(4 * h, 4), pl.ds(4 * h, 2), pl.ds(4 * h + 2, 2)
-        sent = []
         for i, sign, quarter in ((0, 1, front), (1, -1, back)):
-            arrive((far[i], far[2 + i]))
+            arrive(far[i])
             sb[slot, i, whole] = part(2 * sign)[whole] + a1[slot, i, whole]
             sb[slot, i, quarter] = sb[slot, i, quarter] + a2[slot, i, quarter]
-            sent.append(remote(sb.at[slot, i, whole], b2.at[slot, i, whole], peer(2 * sign)))
-        return tuple(sent)
-
-    def scatter_near(part, slot, h):
+            remote(sb.at[slot, i, whole], b2.at[slot, i, whole], peer(2 * sign), last)
+
+    def scatter_near(part, slot, h, last):
         whole = pl.ds(4 * h, 4)
-        return (
-            remote(part(1).at[whole], d1.at[slot, 0, whole], peer(1)),
-            remote(part(-1).at[whole], d1.at[slot, 1, whole], peer(-1)),
-        )
-
-    def scatter_sum(part, slot, h, copies):
+        remote(part(1).at[whole], d1.at[slot, 0, whole], peer(1), last)
+        remote(part(-1).at[whole], d1.at[slot, 1, whole], peer(-1), last)
+
+    def scatter_sum(part, slot, h, last):
         whole = pl.ds(4 * h, 4)
-        arrive(copies)
+        arrive(last)
         return (
             part(0)[whole]
             + (d1[slot, 0, whole] + d1[slot, 1, whole])
             + (b2[slot, 0, whole] + b2[slot, 1, whole])
         )
 
-    def give(shard, k, to, planes):
+    def give(shard, k, to, planes, group):
         ref = shard(k).at[planes]
-        return remote(ref, ref, peer(to))
+        remote(ref, ref, peer(to), group)
 
     def gather_two(shard, h):
         whole = pl.ds(4 * h, 4)
-        return give(shard, 0, 2, whole), give(shard, 0, -2, whole)
-
-    def gather_one(shard, h):
+        two = new(), new()
+        give(shard, 0, 2, whole, two[0])
+        give(shard, 0, -2, whole, two[1])
+        return two
+
+    def gather_one(shard, h, group):
         whole = pl.ds(4 * h, 4)
-        return give(shard, 0, 1, whole), give(shard, 0, -1, whole)
-
-    def gather_on(shard, h, two, arrived=lambda k, h: None):
+        give(shard, 0, 1, whole, group)
+        give(shard, 0, -1, whole, group)
+
+    def gather_on(shard, h, two, three, four, arrived=lambda k, h: None):
         whole, front, back = pl.ds(4 * h, 4), pl.ds(4 * h, 2), pl.ds(4 * h + 2, 2)
-        arrive(two[:1])
-        ahead = give(shard, -2, 2, front), give(shard, -2, 1, whole)
+        arrive(two[0])
+        give(shard, -2, 2, front, four)
+        give(shard, -2, 1, whole, three)
         arrived(-2, h)
-        arrive(two[1:])
-        behind = give(shard, 2, -2, back), give(shard, 2, -1, whole)
+        arrive(two[1])
+        give(shard, 2, -2, back, four)
+        give(shard, 2, -1, whole, three)
         arrived(2, h)
-        return ahead + behind
 
     order = (4, 3, -3, 2, -2, 1, -1, 0)
 
-    def to_twin(k, parity):
-        ref = x2.at[q, 2 * chip(k) + parity]
-        return remote(ref, ref, sibling)
-
-    wanted = [to_twin(k, 1 - q) for k in order]
+    def to_twin(ks, parity):
+        group = new()
+        for k in ks:
+            ref = x2.at[q, 2 * chip(k) + parity]
+            remote(ref, ref, sibling, group)
+        return group
+
+    wanted = to_twin(order[:3], 1 - q), to_twin(order[3:], 1 - q)
 
     block = block_ref[0]
     root_core = lax.rem(block, 2)
@@ -165,30 +187,35 @@
     def masked(k):
         return mask.at[chip(k)]
 
-    def fill(pairs):
-        for k, copy in pairs:
-            copy.wait_recv()
+    def fill(ks, copies):
+        arrive(copies)
+        for k in ks:
             i = 2 * chip(k) + q
             mine = jnp.where(root_core == 0, x2[0, i], x2[1, i])
             mask[chip(k)] = jnp.where(is_root, mine, 0.0)
 
-    pairs = list(zip(order, wanted))
-    fill(pairs[:3])
+    fill(order[:3], wanted[0])
+    phase[0] = 1
     far = [scatter_far(masked, 0, h) for h in range(2)]
-    fill(pairs[3:])
-    near = [scatter_near(masked, 0, h) for h in range(2)]
-    others = [to_twin(k, q) for k in order]
-    mid = [scatter_mid(masked, 0, h, far[h]) for h in range(2)]
-
-    halo = []
+    fill(order[3:], wanted[1])
+    last = [new(), new()]
+    for h in range(2):
+        scatter_near(masked, 0, h, last[h])
+    others = to_twin(order, q)
+    for h in range(2):
+        scatter_mid(masked, 0, h, far[h], last[h])
+
+    phase[0] = 2
+    halo = new()
 
     def lend(first, planes, to, shift):
-        halo.append(remote(act.at[pl.ds(first, planes)], act.at[pl.ds(first + shift, planes)], side(to)))
-
-    act[pl.ds(HALO, 4)] = scatter_sum(masked, 0, 0, near[0] + mid[0])
+        src, dst = act.at[pl.ds(first, planes)], act.at[pl.ds(first + shift, planes)]
+        remote(src, dst, side(to), halo)
+
+    act[pl.ds(HALO, 4)] = scatter_sum(masked, 0, 0, last[0])
     lend(HALO, 4, -1, NX)
     lend(HALO + 2, 2, 1, -NX)
-    act[pl.ds(HALO + 4, 4)] = scatter_sum(masked, 0, 1, near[1] + mid[1])
+    act[pl.ds(HALO + 4, 4)] = scatter_sum(masked, 0, 1, last[1])
     lend(HALO + 4, 2, -1, NX)
     lend(HALO + 4, 4, 1, -NX)
 
@@ -207,10 +234,11 @@
         packed[j] = both[:, :128]
         packed[j + 1] = both[:, 128:]
     panels[orb] = packed[orb]
-    panel_copies = []
+    panel_copies = new(panels.at[pl.ds(0, NORB - 1)])
+    sent[6]["span"] = panel_copies["span"]
     for k in range(1, NORB):
         to = lax.rem(orb + k, NORB)
-        panel_copies.append(remote(packed.at[to], panels.at[orb], (dom, to)))
+        remote(packed.at[to], panels.at[orb], (dom, to), panel_copies, sent[6])
 
     field = act[pl.ds(HALO, NX)]
     inner = (pot[...] - 1.5 * CENTER) * field
@@ -266,7 +294,11 @@
         summed = dot_nn(s_both, jnp.where(of_orbital, 1.0, 0.0).astype(BF))
         pbuf[batch, dom] = summed[:4] + summed[4:]
         ref = pbuf.at[batch, dom]
-        return [remote(ref, ref, side(k)) for k in range(1, NDOM)]
+        sums = new(pbuf.at[batch, pl.ds(0, NDOM - 1)])
+        sent[7 + batch]["span"] = sums["span"]
+        for k in range(1, NDOM):
+            remote(ref, ref, side(k), sums, sent[7 + batch])
+        return sums
 
     def remove(batch, ks, copies, halves):
         rows = len(ks) * NY
@@ -292,13 +324,16 @@
             if x == 2 or x == 6:
                 halves(x // 4)
 
-    one = [gather_one(shard, 0), gather_one(shard, 1)]
+    phase[0] = 3
+    one, on = new(), new()
+    gather_one(shard, 0, one)
+    gather_one(shard, 1, one)
     two = [gather_two(shard, 0), gather_two(shard, 1)]
-    arrive(one[0] + one[1])
+    arrive(one)
     batches = ((0, 1, -1), (2, -2), (3, -3, 4))
     sums = [project(0, batches[0])]
-    on = [gather_on(shard, 0, two[0])]
-    on.append(gather_on(shard, 1, two[1]))
+    gather_on(shard, 0, two[0], on, on)
+    gather_on(shard, 1, two[1], on, on)
     sums.append(project(1, batches[1]))
 
     def removed(k):
@@ -307,25 +342,28 @@
     def owned(k):
         return grad.at[2 * chip(k + 4) + q]
 
-    far, mid, near, twins = [], [], [], [[], []]
+    phase[0] = 4
+    far, last, twins = [], [new(), new()], [new(), new()]
     remove(0, batches[0], sums[0], lambda h: far.append(scatter_far(removed, 1, h)))
-    arrive(on[0] + on[1])
+    arrive(on)
     sums.append(project(2, batches[2]))
     remove(1, batches[1], sums[1], lambda h: None)
-    mid.append(scatter_mid(removed, 1, 0, far[0]))
-    mid.append(scatter_mid(removed, 1, 1, far[1]))
-    remove(2, batches[2], sums[2], lambda h: near.append(scatter_near(removed, 1, h)))
+    for h in range(2):
+        scatter_mid(removed, 1, h, far[h], last[h])
+    remove(2, batches[2], sums[2], lambda h: scatter_near(removed, 1, h, last[h]))
+
+    phase[0] = 5
 
     def to_sibling(k, h):
         ref = owned(k).at[pl.ds(4 * h, 4)]
-        twins[h].append(remote(ref, ref, sibling))
-
-    two, one, on = [], [], []
+        remote(ref, ref, sibling, twins[h])
+
+    two, one, three, four = [], [new(), new()], [new(), new()], [new(), new()]
     for h in range(2):
         half = pl.ds(4 * h, 4)
-        owned(0)[half] = amat[chip(4), half] - scatter_sum(removed, 1, h, near[h] + mid[h])
+        owned(0)[half] = amat[chip(4), half] - scatter_sum(removed, 1, h, last[h])
         two.append(gather_two(owned, h))
-        one.append(gather_one(owned, h))
+        gather_one(owned, h, one[h])
         to_sibling(0, h)
 
     arrive(panel_copies)
@@ -349,25 +387,25 @@
     upd[:, 4:] = x2[q, :, 4:]
 
     for h in range(2):
-        on.append(gather_on(owned, h, two[h], to_sibling))
-    for h in range(2):
-        for i, k in ((0, -1), (1, 1)):
-            arrive(one[h][i : i + 1])
-            to_sibling(k, h)
-    for h in range(2):
-        arrive(on[h][1:2])
+        gather_on(owned, h, two[h], three[h], four[h], to_sibling)
+    for h in range(2):
+        arrive(one[h])
+        to_sibling(-1, h)
+        to_sibling(1, h)
+    for h in range(2):
+        arrive(three[h])
         to_sibling(-3, h)
-        arrive(on[h][3:4])
         to_sibling(3, h)
-        arrive((on[h][0], on[h][2]))
+        arrive(four[h])
         to_sibling(4, h)
 
     arrive(twins[0])
     for x in range(0, 4, 2):
         update(grad, w_both, x2.at[q], upd, x, x)
     arrive(twins[1])
-    for copy in started:
-        copy.wait_send()
+    for group in sent:
+        span(group).wait_send()
+    assert next(groups) == recv.shape[0]
 
 
 def update(grad, w_both, old, new, x, at):
@@ -418,9 +456,9 @@
         pltpu.VMEM((2, 2, *shard), F32),
         pltpu.VMEM((2, 2, *shard), F32),
         pltpu.VMEM((2, 2, *shard), F32),
-        pltpu.SemaphoreType.DMA((160,)),
-        pltpu.SemaphoreType.DMA((160,)),
-        pltpu.SemaphoreType.DMA((8,)),
+        pltpu.SemaphoreType.DMA((10,)),
+        pltpu.SemaphoreType.DMA((38,)),
+        pltpu.SemaphoreType.DMA((3,)),
     ]
     hbm = pl.BlockSpec(memory_space=pl.ANY)
     smem = pl.BlockSpec(memory_space=pltpu.SMEM)

time: 64.2 us -> 61.5 us (0.958)
  Pallas kernels: 62.1 us -> 59.5 us
    pallas_call x1, Pallas kernels: 60.8 us -> 58.1 us  [per_device(): pl.pallas_call(kernel, out_shape=(whole, jax.ShapeDtypeStruct((2 * NB * N...]
where the time goes in v4:
time: 61.5 us; the launch traced here: 61.4 us
  Pallas kernels  59.5 us (97%)
  between operations  1.93 us (3%)
    pallas_call x1, Pallas kernels, per_device(): pl.pallas_call(kernel, out_shape=(whole, jax.ShapeDtypeStruct((2 * NB * N...  58.1 us
    pallas_call x1, Pallas kernels, per_device(): pl.pallas_call(update_kernel, out_shape=(whole, whole), in_specs=[vmem, v...  1.37 us

profile of v4, /device:TPU:1, one launch (start us, length us, event | category | flops | bytes accessed | tf_op | source)
XLA Modules:
  0.0 61.4 jit_solution(17417820162685431742)
XLA Ops:
  1.9 58.1 %gradient.1 = (f32[16,8,16,128]{3,2,1,0:T(8,128)S(1)}, bf16[512,256]{1,0:T(8,128)(2,1)S(1)}, f32[16,8,16,128]{3,2,1,0:T(8,128)S(1)}) custom-call(s32[1]{0:T(128)S(6)} %copy.7.block_ref, s32[1]{0:T(128)S(6)} %copy.8.owner_ref, f32[16,8,16,128]{3,2,1,0:T(8,128)} %x_hbm.1, f32[8,16,128]{2,1,0:T(8,128)} %pot_hbm.1, f32[16,256]{1,0:T(8,128)} %rot_hbm.1), custom_call_target="tpu_custom_call" | custom-call | flops 268435456 | bytes 3145728 | tf_op jit(solution)/shard_map/gradient/pallas_call | solution.py:468
  60.0 1.4 %update.1 = (f32[16,8,16,128]{3,2,1,0:T(8,128)}, f32[16,8,16,128]{3,2,1,0:T(8,128)}) custom-call(f32[16,8,16,128]{3,2,1,0:T(8,128)S(1)} %get-tuple-element.5.grad, bf16[512,256]{1,0:T(8,128)(2,1)S(1)} %get-tuple-element.6.w_ref, f32[16,8,16,128]{3,2,1,0:T(8,128)S(1)} %get-tuple-element.7.upd), custom_call_target="tpu_custom_call" | custom-call | flops 268435456 | bytes 4194304 | tf_op jit(solution)/shard_map/update/pallas_call | solution.py:480

commit v5 on v4

--- a/solution.py
+++ b/solution.py
@@ -1,3 +1,4 @@
+import functools
 import itertools
 import math
 
@@ -39,10 +40,58 @@
     return row_of(rows) == col_of(cols)
 
 
+def scatter_kernel(root, x_hbm, mine, sems):
+    dom = lax.axis_index("dom")
+    orb = lax.axis_index("orb")
+    chip, core = root // 2, root % 2
+    barrier = pltpu.get_barrier_semaphore()
+
+    def send(c):
+        return pltpu.make_async_remote_copy(
+            src_ref=x_hbm.at[c], dst_ref=mine, send_sem=sems.at[0], recv_sem=sems.at[1],
+            device_id=(dom, c), device_id_type=MESH,
+        )
+
+    @pl.when(orb == root)
+    def _():
+        pl.semaphore_wait(barrier, NORB - 1)
+        for k in (4, 3, -3, 2, -2, 1, -1, 0):
+            for c in (2 * ((chip + k) % NCHIP), 2 * ((chip + k) % NCHIP) + 1):
+                if c != root:
+                    send(c).start()
+        own = pltpu.make_async_copy(x_hbm.at[root], mine, sems.at[2])
+        own.start()
+        own.wait()
+        rest = x_hbm.at[pl.ds(0, NORB - 1)]
+        pltpu.make_async_remote_copy(
+            src_ref=rest, dst_ref=rest, send_sem=sems.at[0], recv_sem=sems.at[1],
+            device_id=(dom, 2 * chip + 1 - core), device_id_type=MESH,
+        ).wait_send()
+
+    @pl.when(orb != root)
+    def _():
+        pl.semaphore_signal(barrier, inc=1, device_id=(dom, root), device_id_type=MESH)
+        send(root).wait_recv()
+
+
+def scattered(root, x_hbm):
+    return pl.pallas_call(
+        functools.partial(scatter_kernel, root),
+        out_shape=jax.ShapeDtypeStruct((NX, NY, NZ), F32),
+        in_specs=[pl.BlockSpec(memory_space=pl.ANY)],
+        out_specs=pl.BlockSpec(memory_space=pltpu.VMEM),
+        scratch_shapes=[pltpu.SemaphoreType.DMA((3,))],
+        compiler_params=pltpu.CompilerParams(
+            collective_id=root, has_side_effects=True, vmem_limit_bytes=40 << 20
+        ),
+        name="scatter",
+    )(pltpu.with_memory_space_constraint(x_hbm, pltpu.HBM))
+
+
 def kernel(
-    block_ref, owner_ref, x_hbm, pot_hbm, rot_hbm, grad, w_ref, upd,
-    x2, xh, xl, pot, rot, mask, remo, act, amat, pbuf, packed, panels,
-    a1, a2, d1, b2, sb, send, recv, loc,
+    owner_ref, mine, x_hbm, pot_hbm, rot_hbm, grad, w_ref, upd,
+    x2, xh, xl, pot, rot, remo, act, amat, pbuf, packed, panels,
+    a1, a2, d1, b2, sb, send, recv, loc, greetings,
 ):
     dom = lax.axis_index("dom")
     orb = lax.axis_index("orb")
@@ -98,18 +147,24 @@
         for i, (src, dst) in enumerate(((x_hbm, x2.at[q]), (pot_hbm, pot), (rot_hbm, rot)))
     ]
     loads[0].start()
+    row, col = lax.div(dom, 4), lax.rem(dom, 4)
+    around = [
+        (4 * lax.rem(row + i, 4) + lax.rem(col + j, 4), orb) for i, j in ((0, 1), (0, 3), (1, 0), (3, 0))
+    ]
+    near = [peer(2), peer(-2), side(1), side(-1), *around, peer(1), peer(-1), sibling]
     barrier = pltpu.get_barrier_semaphore()
-    for k in (8, 9, 7, 10, 6, 11, 5, 12, 4, 13, 3, 14, 2, 15, 1):
-        pl.semaphore_signal(
-            barrier, inc=1, device_id=(dom, lax.rem(orb + k, NORB)), device_id_type=MESH
-        )
-    for k in range(1, NDOM):
-        pl.semaphore_signal(barrier, inc=1, device_id=side(k), device_id_type=MESH)
+    for device in near:
+        pl.semaphore_signal(barrier, inc=1, device_id=device, device_id_type=MESH)
     for copy in loads[1:]:
         copy.start()
-    for copy in loads:
-        copy.wait()
-    pl.semaphore_wait(barrier, NDOM + NORB - 2)
+    pl.semaphore_wait(barrier, len(near))
+
+    def greet(i):
+        if i > 0:
+            pl.semaphore_wait(greetings.at[i - 1], len(around))
+        if i < 3:
+            for device in around:
+                pl.semaphore_signal(greetings.at[i], inc=1, device_id=device, device_id_type=MESH)
 
     def scatter_far(part, slot, h):
         whole, front, back = pl.ds(4 * h, 4), pl.ds(4 * h, 2), pl.ds(4 * h + 2, 2)
@@ -169,55 +224,22 @@
         give(shard, 2, -1, whole, three)
         arrived(2, h)
 
-    order = (4, 3, -3, 2, -2, 1, -1, 0)
-
-    def to_twin(ks, parity):
-        group = new()
-        for k in ks:
-            ref = x2.at[q, 2 * chip(k) + parity]
-            remote(ref, ref, sibling, group)
-        return group
-
-    wanted = to_twin(order[:3], 1 - q), to_twin(order[3:], 1 - q)
-
-    block = block_ref[0]
-    root_core = lax.rem(block, 2)
-    is_root = lax.div(block, 2) == z
-
-    def masked(k):
-        return mask.at[chip(k)]
-
-    def fill(ks, copies):
-        arrive(copies)
-        for k in ks:
-            i = 2 * chip(k) + q
-            mine = jnp.where(root_core == 0, x2[0, i], x2[1, i])
-            mask[chip(k)] = jnp.where(is_root, mine, 0.0)
-
-    fill(order[:3], wanted[0])
     phase[0] = 1
-    far = [scatter_far(masked, 0, h) for h in range(2)]
-    fill(order[3:], wanted[1])
-    last = [new(), new()]
-    for h in range(2):
-        scatter_near(masked, 0, h, last[h])
-    others = to_twin(order, q)
-    for h in range(2):
-        scatter_mid(masked, 0, h, far[h], last[h])
-
-    phase[0] = 2
     halo = new()
 
     def lend(first, planes, to, shift):
-        src, dst = act.at[pl.ds(first, planes)], act.at[pl.ds(first + shift, planes)]
+        src, dst = mine.at[pl.ds(first, planes)], act.at[pl.ds(first + shift, planes)]
         remote(src, dst, side(to), halo)
 
-    act[pl.ds(HALO, 4)] = scatter_sum(masked, 0, 0, last[0])
-    lend(HALO, 4, -1, NX)
-    lend(HALO + 2, 2, 1, -NX)
-    act[pl.ds(HALO + 4, 4)] = scatter_sum(masked, 0, 1, last[1])
-    lend(HALO + 4, 2, -1, NX)
-    lend(HALO + 4, 4, 1, -NX)
+    lend(0, HALO, -1, HALO + NX)
+    lend(NX - HALO, HALO, 1, HALO - NX)
+    greet(0)
+    for copy in loads:
+        copy.wait()
+    phase[0] = 0
+    others = new()
+    remote(x2.at[q], x2.at[q], sibling, others)
+    act[pl.ds(HALO, NX)] = mine[...]
 
     r_high, r_low = split(rot[...])
     r_both = jnp.concatenate([r_high, r_low], 0)
@@ -234,12 +256,7 @@
         packed[j] = both[:, :128]
         packed[j + 1] = both[:, 128:]
     panels[orb] = packed[orb]
-    panel_copies = new(panels.at[pl.ds(0, NORB - 1)])
-    sent[6]["span"] = panel_copies["span"]
-    for k in range(1, NORB):
-        to = lax.rem(orb + k, NORB)
-        remote(packed.at[to], panels.at[orb], (dom, to), panel_copies, sent[6])
-
+    greet(1)
     field = act[pl.ds(HALO, NX)]
     inner = (pot[...] - 1.5 * CENTER) * field
     for k in range(1, 7):
@@ -248,6 +265,7 @@
             + pltpu.roll(field, k, 2) + pltpu.roll(field, NZ - k, 2)
         )
         inner = inner - (0.5 * SIDES[k - 1]) * near
+    greet(2)
     arrive(others)
     for j in range(2):
         def cast(a, carry, j=j):
@@ -295,9 +313,9 @@
         pbuf[batch, dom] = summed[:4] + summed[4:]
         ref = pbuf.at[batch, dom]
         sums = new(pbuf.at[batch, pl.ds(0, NDOM - 1)])
-        sent[7 + batch]["span"] = sums["span"]
+        sent[6 + batch]["span"] = sums["span"]
         for k in range(1, NDOM):
-            remote(ref, ref, side(k), sums, sent[7 + batch])
+            remote(ref, ref, side(k), sums, sent[6 + batch])
         return sums
 
     def remove(batch, ks, copies, halves):
@@ -324,11 +342,12 @@
             if x == 2 or x == 6:
                 halves(x // 4)
 
-    phase[0] = 3
+    phase[0] = 2
     one, on = new(), new()
     gather_one(shard, 0, one)
     gather_one(shard, 1, one)
     two = [gather_two(shard, 0), gather_two(shard, 1)]
+    greet(3)
     arrive(one)
     batches = ((0, 1, -1), (2, -2), (3, -3, 4))
     sums = [project(0, batches[0])]
@@ -342,17 +361,22 @@
     def owned(k):
         return grad.at[2 * chip(k + 4) + q]
 
-    phase[0] = 4
+    phase[0] = 3
     far, last, twins = [], [new(), new()], [new(), new()]
     remove(0, batches[0], sums[0], lambda h: far.append(scatter_far(removed, 1, h)))
     arrive(on)
     sums.append(project(2, batches[2]))
+    panel_copies = new(panels.at[pl.ds(0, NORB - 1)])
+    sent[5]["span"] = panel_copies["span"]
+    for k in range(1, NORB):
+        to = lax.rem(orb + k, NORB)
+        remote(packed.at[to], panels.at[orb], (dom, to), panel_copies, sent[5])
     remove(1, batches[1], sums[1], lambda h: None)
     for h in range(2):
         scatter_mid(removed, 1, h, far[h], last[h])
     remove(2, batches[2], sums[2], lambda h: scatter_near(removed, 1, h, last[h]))
 
-    phase[0] = 5
+    phase[0] = 4
 
     def to_sibling(k, h):
         ref = owned(k).at[pl.ds(4 * h, 4)]
@@ -445,7 +469,6 @@
         pltpu.VMEM(shard, F32),
         pltpu.VMEM((NB, NB * NORB), F32),
         pltpu.VMEM((NCHIP, *shard), F32),
-        pltpu.VMEM((NCHIP, *shard), F32),
         pltpu.VMEM((NX + 2 * HALO, NY, NZ), F32),
         pltpu.VMEM((NCHIP, *shard), F32),
         pltpu.VMEM((3, NDOM, 4, 128), F32),
@@ -456,27 +479,30 @@
         pltpu.VMEM((2, 2, *shard), F32),
         pltpu.VMEM((2, 2, *shard), F32),
         pltpu.VMEM((2, 2, *shard), F32),
-        pltpu.SemaphoreType.DMA((10,)),
-        pltpu.SemaphoreType.DMA((38,)),
+        pltpu.SemaphoreType.DMA((9,)),
+        pltpu.SemaphoreType.DMA((30,)),
         pltpu.SemaphoreType.DMA((3,)),
+        pltpu.SemaphoreType.REGULAR((3,)),
     ]
     hbm = pl.BlockSpec(memory_space=pl.ANY)
     smem = pl.BlockSpec(memory_space=pltpu.SMEM)
     vmem = pl.BlockSpec(memory_space=pltpu.VMEM)
     whole = jax.ShapeDtypeStruct((NB, *shard), F32)
-    arrays = (pltpu.with_memory_space_constraint(v, pltpu.HBM) for v in (orbitals, potential, rotation))
+    x_hbm = pltpu.with_memory_space_constraint(orbitals, pltpu.HBM)
+    arrays = (pltpu.with_memory_space_constraint(v, pltpu.HBM) for v in (potential, rotation))
+    mine = lax.switch(block[0], [functools.partial(scattered, r) for r in range(NORB)], x_hbm)
     gradient, weights, updated = pl.pallas_call(
         kernel,
         out_shape=(whole, jax.ShapeDtypeStruct((2 * NB * NY, NB * NY), BF), whole),
-        in_specs=[smem, smem, hbm, hbm, hbm],
+        in_specs=[smem, vmem, hbm, hbm, hbm],
         out_specs=(vmem, vmem, vmem),
         scratch_shapes=scratch,
         compiler_params=pltpu.CompilerParams(
-            collective_id=0, has_side_effects=True, vmem_limit_bytes=40 << 20
+            collective_id=NORB, has_side_effects=True, vmem_limit_bytes=40 << 20
         ),
         cost_estimate=pl.CostEstimate(flops=1 << 28, bytes_accessed=3 << 20, transcendentals=0),
         name="gradient",
-    )(block, owner, *arrays)
+    )(owner, mine, x_hbm, *arrays)
     return pl.pallas_call(
         update_kernel,
         out_shape=(whole, whole),

time: 61.5 us -> 59.9 us (0.974)
  Pallas kernels: 59.5 us -> 57.8 us
    pallas_call x1, Pallas kernels: 58.1 us -> 43.2 us  [per_device(): pl.pallas_call(kernel, out_shape=(whole, jax.ShapeDtypeStruct((2 * NB * N...]
    pallas_call x0 -> x1, Pallas kernels: none -> 13.3 us  [scattered(): pl.pallas_call(functools.partial(scatter_kernel, root), out_shape=jax.Sha...]
where the time goes in v5:
time: 59.9 us; the launch traced here: 59.8 us
  Pallas kernels  57.8 us (96%)
  between operations  1.94 us (3%)
    pallas_call x1, Pallas kernels, per_device(): pl.pallas_call(kernel, out_shape=(whole, jax.ShapeDtypeStruct((2 * NB * N...  43.2 us
    pallas_call x1, Pallas kernels, scattered(): pl.pallas_call(functools.partial(scatter_kernel, root), out_shape=jax.Sha...  13.3 us
    pallas_call x1, Pallas kernels, per_device(): pl.pallas_call(update_kernel, out_shape=(whole, whole), in_specs=[vmem, v...  1.37 us

profile of v5, /device:TPU:1, one launch (start us, length us, event | category | flops | bytes accessed | tf_op | source)
XLA Modules:
  0.0 59.8 jit_solution(1437568614721546731)
XLA Ops:
  1.9 13.3 %conditional.1 = (f32[8,16,128]{2,1,0:T(8,128)S(1)}) conditional(s32[]{:T(128)} %bitcast, f32[16,8,16,128]{3,2,1,0:T(8,128)} %x_hbm.17, f32[16,8,16,128]{3,2,1,0:T(8,128)} %x_hbm.17, f32[16,8,16,128]{3,2,1,0:T(8,128)} %x_hbm.17, f32[16,8,16,128]{3,2,1,0:T(8,128)} %x_hbm.17, f32[16,8,16,128]{3,2,1,0:T(8,128)} %x_hbm.17, ...), branch_computations={%region_0.0_spmd, %region_1.0_spmd, %region_2.0_spmd, %region_3.0_... | conditional | bytes 8 | solution.py:493
  2.0 13.3 %scatter.24 = f32[8,16,128]{2,1,0:T(8,128)S(1)} custom-call(f32[16,8,16,128]{3,2,1,0:T(8,128)} %x_hbm.9), custom_call_target="tpu_custom_call" | custom-call | tf_op jit(solution)/shard_map/cond/branch_8_fun/scatter/pallas_call | solution.py:78
  15.3 43.2 %gradient.1 = (f32[16,8,16,128]{3,2,1,0:T(8,128)S(1)}, bf16[512,256]{1,0:T(8,128)(2,1)S(1)}, f32[16,8,16,128]{3,2,1,0:T(8,128)S(1)}) custom-call(s32[1]{0:T(128)S(6)} %copy.24.owner_ref, f32[8,16,128]{2,1,0:T(8,128)S(1)} %get-tuple-element.41.mine, f32[16,8,16,128]{3,2,1,0:T(8,128)} %x_hbm.17, f32[8,16,128]{2,1,0:T(8,128)} %pot_hbm.1, f32[16,256]{1,0:T(8,128)} %rot_hbm.1), custom_call_target="tpu_custom_call" | custom-call | flops 268435456 | bytes 3145728 | tf_op jit(solution)/shard_map/gradient/pallas_call | solution.py:494
  58.4 1.4 %update.1 = (f32[16,8,16,128]{3,2,1,0:T(8,128)}, f32[16,8,16,128]{3,2,1,0:T(8,128)}) custom-call(f32[16,8,16,128]{3,2,1,0:T(8,128)S(1)} %get-tuple-element.38.grad, bf16[512,256]{1,0:T(8,128)(2,1)S(1)} %get-tuple-element.39.w_ref, f32[16,8,16,128]{3,2,1,0:T(8,128)S(1)} %get-tuple-element.40.upd), custom_call_target="tpu_custom_call" | custom-call | flops 268435456 | bytes 4194304 | tf_op jit(solution)/shard_map/update/pallas_call | solution.py:506

commit v6 on v4

--- a/solution.py
+++ b/solution.py
@@ -41,7 +41,7 @@
 
 def kernel(
     block_ref, owner_ref, x_hbm, pot_hbm, rot_hbm, grad, w_ref, upd,
-    x2, xh, xl, pot, rot, mask, remo, act, amat, pbuf, packed, panels,
+    x2, xh, xl, pot, rot, mask, remo, act, ham, amat, pout, pbuf, packed, panels,
     a1, a2, d1, b2, sb, send, recv, loc,
 ):
     dom = lax.axis_index("dom")
@@ -58,7 +58,11 @@
     def side(k):
         return (lax.rem(dom + (k + NDOM), NDOM), orb)
 
-    sibling = (dom, orb + 1 - 2 * q)
+    twin = orb + 1 - 2 * q
+    sibling = (dom, twin)
+
+    def across(k):
+        return (lax.rem(dom + k, NDOM), twin)
     groups = itertools.count()
     sent = [dict(sem=i, rows=0) for i in range(send.shape[0])]
     phase = [0]
@@ -104,12 +108,14 @@
             barrier, inc=1, device_id=(dom, lax.rem(orb + k, NORB)), device_id_type=MESH
         )
     for k in range(1, NDOM):
+        pl.semaphore_signal(barrier, inc=1, device_id=across(k), device_id_type=MESH)
+    for k in (1, -1):
         pl.semaphore_signal(barrier, inc=1, device_id=side(k), device_id_type=MESH)
     for copy in loads[1:]:
         copy.start()
     for copy in loads:
         copy.wait()
-    pl.semaphore_wait(barrier, NDOM + NORB - 2)
+    pl.semaphore_wait(barrier, NDOM + NORB)
 
     def scatter_far(part, slot, h):
         whole, front, back = pl.ds(4 * h, 4), pl.ds(4 * h, 2), pl.ds(4 * h + 2, 2)
@@ -292,12 +298,11 @@
         of_orbital = indicator((cols, 128), lambda r: r >> 4, lambda c: c)
         s_both = jnp.concatenate(split(summed), 0)
         summed = dot_nn(s_both, jnp.where(of_orbital, 1.0, 0.0).astype(BF))
-        pbuf[batch, dom] = summed[:4] + summed[4:]
-        ref = pbuf.at[batch, dom]
-        sums = new(pbuf.at[batch, pl.ds(0, NDOM - 1)])
+        pout[batch] = summed[:4] + summed[4:]
+        sums = new(pbuf.at[batch])
         sent[7 + batch]["span"] = sums["span"]
-        for k in range(1, NDOM):
-            remote(ref, ref, side(k), sums, sent[7 + batch])
+        for k in range(NDOM):
+            remote(pout.at[batch], pbuf.at[batch, dom], across(k), sums, sent[7 + batch])
         return sums
 
     def remove(batch, ks, copies, halves):
@@ -340,12 +345,14 @@
         return remo.at[chip(k + 4)]
 
     def owned(k):
-        return grad.at[2 * chip(k + 4) + q]
+        return grad.at[2 * chip(k + 4) + 1 - q]
 
     phase[0] = 4
     far, last, twins = [], [new(), new()], [new(), new()]
     remove(0, batches[0], sums[0], lambda h: far.append(scatter_far(removed, 1, h)))
     arrive(on)
+    base = new()
+    remote(shard(4), ham, sibling, base)
     sums.append(project(2, batches[2]))
     remove(1, batches[1], sums[1], lambda h: None)
     for h in range(2):
@@ -358,10 +365,11 @@
         ref = owned(k).at[pl.ds(4 * h, 4)]
         remote(ref, ref, sibling, twins[h])
 
+    arrive(base)
     two, one, three, four = [], [new(), new()], [new(), new()], [new(), new()]
     for h in range(2):
         half = pl.ds(4 * h, 4)
-        owned(0)[half] = amat[chip(4), half] - scatter_sum(removed, 1, h, last[h])
+        owned(0)[half] = ham[half] - scatter_sum(removed, 1, h, last[h])
         two.append(gather_two(owned, h))
         gather_one(owned, h, one[h])
         to_sibling(0, h)
@@ -447,7 +455,9 @@
         pltpu.VMEM((NCHIP, *shard), F32),
         pltpu.VMEM((NCHIP, *shard), F32),
         pltpu.VMEM((NX + 2 * HALO, NY, NZ), F32),
+        pltpu.VMEM(shard, F32),
         pltpu.VMEM((NCHIP, *shard), F32),
+        pltpu.VMEM((3, 4, 128), F32),
         pltpu.VMEM((3, NDOM, 4, 128), F32),
         pltpu.VMEM((NORB, 2, 128), F32),
         pltpu.VMEM((NORB, 2, 128), F32),
@@ -457,7 +467,7 @@
         pltpu.VMEM((2, 2, *shard), F32),
         pltpu.VMEM((2, 2, *shard), F32),
         pltpu.SemaphoreType.DMA((10,)),
-        pltpu.SemaphoreType.DMA((38,)),
+        pltpu.SemaphoreType.DMA((39,)),
         pltpu.SemaphoreType.DMA((3,)),
     ]
     hbm = pl.BlockSpec(memory_space=pl.ANY)

time: 61.5 us -> 61 us (level)
  no operation moved by 1% of the time
where the time goes in v6:
time: 61 us; the launch traced here: 60.9 us
  Pallas kernels  59 us (97%)
  between operations  1.93 us (3%)
    pallas_call x1, Pallas kernels, per_device(): pl.pallas_call(kernel, out_shape=(whole, jax.ShapeDtypeStruct((2 * NB * N...  57.6 us
    pallas_call x1, Pallas kernels, per_device(): pl.pallas_call(update_kernel, out_shape=(whole, whole), in_specs=[vmem, v...  1.37 us

profile of v6, /device:TPU:1, one launch (start us, length us, event | category | flops | bytes accessed | tf_op | source)
XLA Modules:
  0.0 60.9 jit_solution(4584302358405360749)
XLA Ops:
  1.9 57.6 %gradient.1 = (f32[16,8,16,128]{3,2,1,0:T(8,128)S(1)}, bf16[512,256]{1,0:T(8,128)(2,1)S(1)}, f32[16,8,16,128]{3,2,1,0:T(8,128)S(1)}) custom-call(s32[1]{0:T(128)S(6)} %copy.7.block_ref, s32[1]{0:T(128)S(6)} %copy.8.owner_ref, f32[16,8,16,128]{3,2,1,0:T(8,128)} %x_hbm.1, f32[8,16,128]{2,1,0:T(8,128)} %pot_hbm.1, f32[16,256]{1,0:T(8,128)} %rot_hbm.1), custom_call_target="tpu_custom_call" | custom-call | flops 268435456 | bytes 3145728 | tf_op jit(solution)/shard_map/gradient/pallas_call | solution.py:478
  59.6 1.4 %update.1 = (f32[16,8,16,128]{3,2,1,0:T(8,128)}, f32[16,8,16,128]{3,2,1,0:T(8,128)}) custom-call(f32[16,8,16,128]{3,2,1,0:T(8,128)S(1)} %get-tuple-element.5.grad, bf16[512,256]{1,0:T(8,128)(2,1)S(1)} %get-tuple-element.6.w_ref, f32[16,8,16,128]{3,2,1,0:T(8,128)S(1)} %get-tuple-element.7.upd), custom_call_target="tpu_custom_call" | custom-call | flops 268435456 | bytes 4194304 | tf_op jit(solution)/shard_map/update/pallas_call | solution.py:490

commit v7 on v6

--- a/solution.py
+++ b/solution.py
@@ -42,7 +42,7 @@
 def kernel(
     block_ref, owner_ref, x_hbm, pot_hbm, rot_hbm, grad, w_ref, upd,
     x2, xh, xl, pot, rot, mask, remo, act, ham, amat, pout, pbuf, packed, panels,
-    a1, a2, d1, b2, sb, send, recv, loc,
+    a1, a2, d1, b2, sb, send, recv, loc, greetings,
 ):
     dom = lax.axis_index("dom")
     orb = lax.axis_index("orb")
@@ -102,20 +102,24 @@
         for i, (src, dst) in enumerate(((x_hbm, x2.at[q]), (pot_hbm, pot), (rot_hbm, rot)))
     ]
     loads[0].start()
+    row, col = lax.div(dom, 4), lax.rem(dom, 4)
+    around = [
+        (4 * lax.rem(row + i, 4) + lax.rem(col + j, 4), orb) for i, j in ((0, 1), (0, 3), (1, 0), (3, 0))
+    ]
+    near = [peer(2), peer(-2), peer(1), peer(-1), sibling, side(1), side(-1), *around]
     barrier = pltpu.get_barrier_semaphore()
-    for k in (8, 9, 7, 10, 6, 11, 5, 12, 4, 13, 3, 14, 2, 15, 1):
-        pl.semaphore_signal(
-            barrier, inc=1, device_id=(dom, lax.rem(orb + k, NORB)), device_id_type=MESH
-        )
-    for k in range(1, NDOM):
-        pl.semaphore_signal(barrier, inc=1, device_id=across(k), device_id_type=MESH)
-    for k in (1, -1):
-        pl.semaphore_signal(barrier, inc=1, device_id=side(k), device_id_type=MESH)
+    for device in near:
+        pl.semaphore_signal(barrier, inc=1, device_id=device, device_id_type=MESH)
     for copy in loads[1:]:
         copy.start()
-    for copy in loads:
-        copy.wait()
-    pl.semaphore_wait(barrier, NDOM + NORB)
+    pl.semaphore_wait(barrier, len(near))
+
+    def greet(i):
+        if i > 0:
+            pl.semaphore_wait(greetings.at[i - 1], len(around))
+        if i < 3:
+            for device in around:
+                pl.semaphore_signal(greetings.at[i], inc=1, device_id=device, device_id_type=MESH)
 
     def scatter_far(part, slot, h):
         whole, front, back = pl.ds(4 * h, 4), pl.ds(4 * h, 2), pl.ds(4 * h + 2, 2)
@@ -180,11 +184,14 @@
     def to_twin(ks, parity):
         group = new()
         for k in ks:
-            ref = x2.at[q, 2 * chip(k) + parity]
-            remote(ref, ref, sibling, group)
+            i = 2 * chip(k) + parity
+            remote(x_hbm.at[i], x2.at[q, i], sibling, group)
         return group
 
     wanted = to_twin(order[:3], 1 - q), to_twin(order[3:], 1 - q)
+
+    for copy in loads:
+        copy.wait()
 
     block = block_ref[0]
     root_core = lax.rem(block, 2)
@@ -203,6 +210,7 @@
     fill(order[:3], wanted[0])
     phase[0] = 1
     far = [scatter_far(masked, 0, h) for h in range(2)]
+    greet(0)
     fill(order[3:], wanted[1])
     last = [new(), new()]
     for h in range(2):
@@ -210,6 +218,8 @@
     others = to_twin(order, q)
     for h in range(2):
         scatter_mid(masked, 0, h, far[h], last[h])
+
+    greet(1)
 
     phase[0] = 2
     halo = new()
@@ -240,12 +250,6 @@
         packed[j] = both[:, :128]
         packed[j + 1] = both[:, 128:]
     panels[orb] = packed[orb]
-    panel_copies = new(panels.at[pl.ds(0, NORB - 1)])
-    sent[6]["span"] = panel_copies["span"]
-    for k in range(1, NORB):
-        to = lax.rem(orb + k, NORB)
-        remote(packed.at[to], panels.at[orb], (dom, to), panel_copies, sent[6])
-
     field = act[pl.ds(HALO, NX)]
     inner = (pot[...] - 1.5 * CENTER) * field
     for k in range(1, 7):
@@ -254,6 +258,7 @@
             + pltpu.roll(field, k, 2) + pltpu.roll(field, NZ - k, 2)
         )
         inner = inner - (0.5 * SIDES[k - 1]) * near
+    greet(2)
     arrive(others)
     for j in range(2):
         def cast(a, carry, j=j):
@@ -262,6 +267,7 @@
             xl[j, a] = low
             return carry
         lax.fori_loop(0, NB, cast, 0)
+    greet(3)
     arrive(halo)
     for k in range(1, 7):
         inner = inner - (0.5 * SIDES[k - 1]) * (act[pl.ds(HALO + k, NX)] + act[pl.ds(HALO - k, NX)])
@@ -354,6 +360,11 @@
     base = new()
     remote(shard(4), ham, sibling, base)
     sums.append(project(2, batches[2]))
+    panel_copies = new(panels.at[pl.ds(0, NORB - 1)])
+    sent[6]["span"] = panel_copies["span"]
+    for k in range(1, NORB):
+        to = lax.rem(orb + k, NORB)
+        remote(packed.at[to], panels.at[orb], (dom, to), panel_copies, sent[6])
     remove(1, batches[1], sums[1], lambda h: None)
     for h in range(2):
         scatter_mid(removed, 1, h, far[h], last[h])
@@ -469,6 +480,7 @@
         pltpu.SemaphoreType.DMA((10,)),
         pltpu.SemaphoreType.DMA((39,)),
         pltpu.SemaphoreType.DMA((3,)),
+        pltpu.SemaphoreType.REGULAR((3,)),
     ]
     hbm = pl.BlockSpec(memory_space=pl.ANY)
     smem = pl.BlockSpec(memory_space=pltpu.SMEM)

time: 61 us -> 60.3 us (0.989)
  Pallas kernels: 59 us -> 58.2 us
    pallas_call x1, Pallas kernels: 57.6 us -> 56.9 us  [per_device(): pl.pallas_call(kernel, out_shape=(whole, jax.ShapeDtypeStruct((2 * NB * N...]
where the time goes in v7:
time: 60.3 us; the launch traced here: 60.2 us
  Pallas kernels  58.2 us (97%)
  between operations  1.93 us (3%)
    pallas_call x1, Pallas kernels, per_device(): pl.pallas_call(kernel, out_shape=(whole, jax.ShapeDtypeStruct((2 * NB * N...  56.9 us
    pallas_call x1, Pallas kernels, per_device(): pl.pallas_call(update_kernel, out_shape=(whole, whole), in_specs=[vmem, v...  1.37 us

profile of v7, /device:TPU:1, one launch (start us, length us, event | category | flops | bytes accessed | tf_op | source)
XLA Modules:
  0.0 60.2 jit_solution(17736916655234111537)
XLA Ops:
  1.9 56.9 %gradient.1 = (f32[16,8,16,128]{3,2,1,0:T(8,128)S(1)}, bf16[512,256]{1,0:T(8,128)(2,1)S(1)}, f32[16,8,16,128]{3,2,1,0:T(8,128)S(1)}) custom-call(s32[1]{0:T(128)S(6)} %copy.7.block_ref, s32[1]{0:T(128)S(6)} %copy.8.owner_ref, f32[16,8,16,128]{3,2,1,0:T(8,128)} %x_hbm.1, f32[8,16,128]{2,1,0:T(8,128)} %pot_hbm.1, f32[16,256]{1,0:T(8,128)} %rot_hbm.1), custom_call_target="tpu_custom_call" | custom-call | flops 268435456 | bytes 3145728 | tf_op jit(solution)/shard_map/gradient/pallas_call | solution.py:490
  58.8 1.4 %update.1 = (f32[16,8,16,128]{3,2,1,0:T(8,128)}, f32[16,8,16,128]{3,2,1,0:T(8,128)}) custom-call(f32[16,8,16,128]{3,2,1,0:T(8,128)S(1)} %get-tuple-element.5.grad, bf16[512,256]{1,0:T(8,128)(2,1)S(1)} %get-tuple-element.6.w_ref, f32[16,8,16,128]{3,2,1,0:T(8,128)S(1)} %get-tuple-element.7.upd), custom_call_target="tpu_custom_call" | custom-call | flops 268435456 | bytes 4194304 | tf_op jit(solution)/shard_map/update/pallas_call | solution.py:502

commit v8 on v7

--- a/solution.py
+++ b/solution.py
@@ -360,14 +360,14 @@
     base = new()
     remote(shard(4), ham, sibling, base)
     sums.append(project(2, batches[2]))
+    remove(1, batches[1], sums[1], lambda h: None)
+    for h in range(2):
+        scatter_mid(removed, 1, h, far[h], last[h])
     panel_copies = new(panels.at[pl.ds(0, NORB - 1)])
     sent[6]["span"] = panel_copies["span"]
     for k in range(1, NORB):
         to = lax.rem(orb + k, NORB)
         remote(packed.at[to], panels.at[orb], (dom, to), panel_copies, sent[6])
-    remove(1, batches[1], sums[1], lambda h: None)
-    for h in range(2):
-        scatter_mid(removed, 1, h, far[h], last[h])
     remove(2, batches[2], sums[2], lambda h: scatter_near(removed, 1, h, last[h]))
 
     phase[0] = 5

time: 60.3 us -> 61.2 us (1.015)
  Pallas kernels: 58.2 us -> 59.2 us
    pallas_call x1, Pallas kernels: 56.9 us -> 57.8 us  [per_device(): pl.pallas_call(kernel, out_shape=(whole, jax.ShapeDtypeStruct((2 * NB * N...]
where the time goes in v8:
time: 61.2 us; the launch traced here: 61.1 us
  Pallas kernels  59.2 us (97%)
  between operations  1.93 us (3%)
    pallas_call x1, Pallas kernels, per_device(): pl.pallas_call(kernel, out_shape=(whole, jax.ShapeDtypeStruct((2 * NB * N...  57.8 us
    pallas_call x1, Pallas kernels, per_device(): pl.pallas_call(update_kernel, out_shape=(whole, whole), in_specs=[vmem, v...  1.37 us

profile of v8, /device:TPU:1, one launch (start us, length us, event | category | flops | bytes accessed | tf_op | source)
XLA Modules:
  0.0 61.1 jit_solution(4050421382718804127)
XLA Ops:
  1.9 57.8 %gradient.1 = (f32[16,8,16,128]{3,2,1,0:T(8,128)S(1)}, bf16[512,256]{1,0:T(8,128)(2,1)S(1)}, f32[16,8,16,128]{3,2,1,0:T(8,128)S(1)}) custom-call(s32[1]{0:T(128)S(6)} %copy.7.block_ref, s32[1]{0:T(128)S(6)} %copy.8.owner_ref, f32[16,8,16,128]{3,2,1,0:T(8,128)} %x_hbm.1, f32[8,16,128]{2,1,0:T(8,128)} %pot_hbm.1, f32[16,256]{1,0:T(8,128)} %rot_hbm.1), custom_call_target="tpu_custom_call" | custom-call | flops 268435456 | bytes 3145728 | tf_op jit(solution)/shard_map/gradient/pallas_call | solution.py:490
  59.7 1.4 %update.1 = (f32[16,8,16,128]{3,2,1,0:T(8,128)}, f32[16,8,16,128]{3,2,1,0:T(8,128)}) custom-call(f32[16,8,16,128]{3,2,1,0:T(8,128)S(1)} %get-tuple-element.5.grad, bf16[512,256]{1,0:T(8,128)(2,1)S(1)} %get-tuple-element.6.w_ref, f32[16,8,16,128]{3,2,1,0:T(8,128)S(1)} %get-tuple-element.7.upd), custom_call_target="tpu_custom_call" | custom-call | flops 268435456 | bytes 4194304 | tf_op jit(solution)/shard_map/update/pallas_call | solution.py:502

commit v9 on v7

--- a/solution.py
+++ b/solution.py
@@ -41,7 +41,7 @@
 
 def kernel(
     block_ref, owner_ref, x_hbm, pot_hbm, rot_hbm, grad, w_ref, upd,
-    x2, xh, xl, pot, rot, mask, remo, act, ham, amat, pout, pbuf, packed, panels,
+    x2, xh, xl, pot, rot, mask, remo, act, ham, amat, pout, pbuf, keep, of_orbital, to_cells, packed, panels,
     a1, a2, d1, b2, sb, send, recv, loc, greetings,
 ):
     dom = lax.axis_index("dom")
@@ -250,6 +250,14 @@
         packed[j] = both[:, :128]
         packed[j + 1] = both[:, 128:]
     panels[orb] = packed[orb]
+    cols = 2 * NB * NY
+    same_y = indicator((3 * NY, cols), lambda r: r & (NY - 1), lambda c: c & (NY - 1))
+    keep[...] = jnp.where(same_y, 1.0, 0.0)
+    pick = indicator((cols, 128), lambda r: r >> 4, lambda c: c)
+    of_orbital[...] = jnp.where(pick, 1.0, 0.0).astype(BF)
+    pick = indicator((128, cols), lambda r: r, lambda c: c >> 4)
+    to_cells[...] = jnp.where(pick, 1.0, 0.0).astype(BF)
+
     field = act[pl.ds(HALO, NX)]
     inner = (pot[...] - 1.5 * CENTER) * field
     for k in range(1, 7):
@@ -273,13 +281,8 @@
         inner = inner - (0.5 * SIDES[k - 1]) * (act[pl.ds(HALO + k, NX)] + act[pl.ds(HALO - k, NX)])
     amat[z] = inner
 
-    cols = 2 * NB * NY
-
     def shard(k):
         return amat.at[chip(k)]
-
-    def same_y(rows):
-        return indicator((rows, cols), lambda r: r & (NY - 1), lambda c: c & (NY - 1))
 
     def x_pairs():
         for x in range(0, NX, 2):
@@ -299,11 +302,10 @@
             a_high, a_low = split(a_pair)
             both = dot_nt(jnp.concatenate([a_high, a_low], 0), h_pair)
             gram = gram + (both[:rows] + both[rows:] + dot_nt(a_high, l_pair))
-        summed = jnp.where(same_y(rows), gram, 0.0).reshape(len(ks), NY, cols).sum(1)
+        summed = jnp.where(keep[:rows] > 0.5, gram, 0.0).reshape(len(ks), NY, cols).sum(1)
         summed = jnp.concatenate([summed, jnp.zeros((4 - len(ks), cols), F32)], 0)
-        of_orbital = indicator((cols, 128), lambda r: r >> 4, lambda c: c)
         s_both = jnp.concatenate(split(summed), 0)
-        summed = dot_nn(s_both, jnp.where(of_orbital, 1.0, 0.0).astype(BF))
+        summed = dot_nn(s_both, of_orbital[...])
         pout[batch] = summed[:4] + summed[4:]
         sums = new(pbuf.at[batch])
         sent[7 + batch]["span"] = sums["span"]
@@ -315,16 +317,12 @@
         rows = len(ks) * NY
         arrive(copies)
         proj = pbuf[batch].sum(0) * (1.0 / (NX * NDOM * NY * NZ))
-        to_rows = indicator((128, cols), lambda r: r, lambda c: c >> 4)
-        spread = dot_nn(
-            jnp.concatenate(split(proj), 0), jnp.where(to_rows, 1.0, 0.0).astype(BF)
-        )
-        keep = same_y(rows)
+        spread = dot_nn(jnp.concatenate(split(proj), 0), to_cells[...])
         weights = []
         for first in (0, 4):
             one = spread[first : first + len(ks)]
             one = jnp.broadcast_to(one[:, None, :], (len(ks), NY, cols)).reshape(rows, cols)
-            weights.append(jnp.where(keep, one, 0.0).astype(BF))
+            weights.append(jnp.where(keep[:rows] > 0.5, one, 0.0).astype(BF))
         k_both = jnp.concatenate(weights, 0)
         for x, h_pair, l_pair in x_pairs():
             both = dot_nn(k_both, h_pair)
@@ -395,9 +393,9 @@
     by_row = dot_nt(jnp.where(of_column, 1.0, 0.0).astype(BF), p_both).astype(BF)
     to_rows = indicator((NB, rows), lambda r: r, lambda c: c >> 4)
     to_rows = jnp.where(to_rows, 1.0, 0.0).astype(BF)
-    keep = indicator((rows, rows), lambda r: r & (NY - 1), lambda c: c & (NY - 1))
+    same_y = indicator((rows, rows), lambda r: r & (NY - 1), lambda c: c & (NY - 1))
     w_high, w_low = (
-        jnp.where(keep, dot_nn(one_of, to_rows), 0.0).astype(BF)
+        jnp.where(same_y, dot_nn(one_of, to_rows), 0.0).astype(BF)
         for one_of in (by_row[:, :NB], by_row[:, NB:])
     )
     w_both = jnp.concatenate([w_high, w_low], 0)
@@ -470,6 +468,9 @@
         pltpu.VMEM((NCHIP, *shard), F32),
         pltpu.VMEM((3, 4, 128), F32),
         pltpu.VMEM((3, NDOM, 4, 128), F32),
+        pltpu.VMEM((3 * NY, 2 * NB * NY), F32),
+        pltpu.VMEM((2 * NB * NY, 128), BF),
+        pltpu.VMEM((128, 2 * NB * NY), BF),
         pltpu.VMEM((NORB, 2, 128), F32),
         pltpu.VMEM((NORB, 2, 128), F32),
         pltpu.VMEM((2, 2, *shard), F32),

time: 60.3 us -> 60.2 us (level)
  no operation moved by 1% of the time
where the time goes in v9:
time: 60.2 us; the launch traced here: 60.1 us
  Pallas kernels  58.2 us (97%)
  between operations  1.93 us (3%)
    pallas_call x1, Pallas kernels, per_device(): pl.pallas_call(kernel, out_shape=(whole, jax.ShapeDtypeStruct((2 * NB * N...  56.8 us
    pallas_call x1, Pallas kernels, per_device(): pl.pallas_call(update_kernel, out_shape=(whole, whole), in_specs=[vmem, v...  1.37 us

profile of v9, /device:TPU:1, one launch (start us, length us, event | category | flops | bytes accessed | tf_op | source)
XLA Modules:
  0.0 60.1 jit_solution(17783822898530468858)
XLA Ops:
  1.9 56.8 %gradient.1 = (f32[16,8,16,128]{3,2,1,0:T(8,128)S(1)}, bf16[512,256]{1,0:T(8,128)(2,1)S(1)}, f32[16,8,16,128]{3,2,1,0:T(8,128)S(1)}) custom-call(s32[1]{0:T(128)S(6)} %copy.7.block_ref, s32[1]{0:T(128)S(6)} %copy.8.owner_ref, f32[16,8,16,128]{3,2,1,0:T(8,128)} %x_hbm.1, f32[8,16,128]{2,1,0:T(8,128)} %pot_hbm.1, f32[16,256]{1,0:T(8,128)} %rot_hbm.1), custom_call_target="tpu_custom_call" | custom-call | flops 268435456 | bytes 3145728 | tf_op jit(solution)/shard_map/gradient/pallas_call | solution.py:491
  58.8 1.4 %update.1 = (f32[16,8,16,128]{3,2,1,0:T(8,128)}, f32[16,8,16,128]{3,2,1,0:T(8,128)}) custom-call(f32[16,8,16,128]{3,2,1,0:T(8,128)S(1)} %get-tuple-element.5.grad, bf16[512,256]{1,0:T(8,128)(2,1)S(1)} %get-tuple-element.6.w_ref, f32[16,8,16,128]{3,2,1,0:T(8,128)S(1)} %get-tuple-element.7.upd), custom_call_target="tpu_custom_call" | custom-call | flops 268435456 | bytes 4194304 | tf_op jit(solution)/shard_map/update/pallas_call | solution.py:503
